TPU v7x, 128 devices: a whole 4x4x4 slice. The times are simulated.
128 devices in a mesh: slab: 64 (over y, x, z), pencil: 2 (over core).
Axes of the slice: x: 4, y: 4, z: 4, core: 2. Of those that a mesh axis runs over, the one named last changes fastest.
Arguments:
- point_feats: bfloat16 [524288, 64], P(('slab', 'pencil')), may hold values from -6 to 6
- point_x: float32 [524288], P(('slab', 'pencil')), may hold values from 0 to 1
- neighbour_dev: int32 [4096, 4], P(('slab', 'pencil')), may hold values from 0 to 127, all different within a row; in each aligned block of 32 rows (0 to 31, 32 to 63, ...) at most 2 rows name the same one
- neighbour_line: int32 [4096, 4], P(('slab', 'pencil')), may hold values from 0 to 127
- spec_weight: bfloat16 [2, 1024, 32, 2, 64, 64], P(None, ('slab', 'pencil')), may hold values from -4.5 to 4.5
- skip_weight: bfloat16 [2, 64, 64], replicated, may hold values from -0.75 to 0.75
Outputs:
- point_out: float32 [524288, 64], P(('slab', 'pencil'))
Inputs may be any that keep to these rules, and one draw needn't show every extreme that they name: `neighbour_dev`: each row names 4 different devices; the rows of one device name any one device at most 2 times, and some device exactly 2 times.
All inputs are finite; a program needn't handle non-finite values.
Results may differ from a plain program's by a relative error of at most 0.003.
Values may be sent and summed in bfloat16 or wider, within the bound.
A program may use at most 192 MiB of HBM per device.

v0:
```python
import jax
import jax.numpy as jnp
from jax import lax
from jax.sharding import PartitionSpec as P

G = 128


dec_scale = 0.5
spread_cells = 0.5
highest = lax.Precision.HIGHEST


def dft_tables(length, n_modes, grid_len, offset):
    cells = jnp.arange(length, dtype=jnp.int32) + offset
    waves = jnp.arange(n_modes, dtype=jnp.int32) - n_modes // 2
    phase = jnp.mod(cells[:, None] * waves[None, :], grid_len).astype(jnp.float32)
    angle = phase * (2.0 * jnp.pi / grid_len)
    return (jnp.cos(angle), jnp.sin(angle))


def kernel_rows(coords, grid_len):
    offset_x = coords[..., None] * grid_len - jnp.arange(grid_len, dtype=jnp.float32)
    return jnp.exp(-offset_x * offset_x / (2.0 * spread_cells * spread_cells)).astype(jnp.bfloat16)


def spectral_layer(field, weight, skip):
    z_slab, y_rows, chans, grid_len = field.shape
    n_modes = weight.shape[1]
    n_slab = lax.axis_size("slab")
    n_pencil = lax.axis_size("pencil")
    pair_count = weight.shape[0]
    all_pairs = n_modes * n_modes
    cos_x, sin_x = dft_tables(grid_len, n_modes, grid_len, 0)
    cos_y, sin_y = dft_tables(y_rows, n_modes, grid_len, lax.axis_index("pencil") * y_rows)
    x_real = jnp.einsum("zycx,xk->zyck", field, cos_x, precision=highest)
    x_imag = -jnp.einsum("zycx,xk->zyck", field, sin_x, precision=highest)
    y_real = jnp.einsum("zyck,yj->zjkc", x_real, cos_y, precision=highest) + jnp.einsum(
        "zyck,yj->zjkc", x_imag, sin_y, precision=highest
    )
    y_imag = jnp.einsum("zyck,yj->zjkc", x_imag, cos_y, precision=highest) - jnp.einsum(
        "zyck,yj->zjkc", x_real, sin_y, precision=highest
    )
    stacked = jnp.stack([y_real, y_imag], axis=3).reshape(z_slab, all_pairs, 2 * chans)
    partial_y = stacked.reshape(z_slab, n_slab, n_pencil, pair_count, 2 * chans)
    summed = lax.psum_scatter(partial_y, "pencil", scatter_dimension=2, tiled=True)
    arrival = lax.all_to_all(summed, "slab", split_axis=1, concat_axis=0, tiled=True)
    columns = arrival.reshape(z_slab * n_slab, pair_count, 2, chans)
    cos_z, sin_z = dft_tables(grid_len, n_modes, grid_len, 0)
    col_real = columns[:, :, 0]
    col_imag = columns[:, :, 1]
    z_real = jnp.einsum("zjc,zm->mjc", col_real, cos_z, precision=highest) + jnp.einsum(
        "zjc,zm->mjc", col_imag, sin_z, precision=highest
    )
    z_imag = jnp.einsum("zjc,zm->mjc", col_imag, cos_z, precision=highest) - jnp.einsum(
        "zjc,zm->mjc", col_real, sin_z, precision=highest
    )
    w_real = weight[:, :, 0].astype(jnp.float32)
    w_imag = weight[:, :, 1].astype(jnp.float32)
    m_real = jnp.einsum("mjc,jmcd->mjd", z_real, w_real, precision=highest) - jnp.einsum(
        "mjc,jmcd->mjd", z_imag, w_imag, precision=highest
    )
    m_imag = jnp.einsum("mjc,jmcd->mjd", z_real, w_imag, precision=highest) + jnp.einsum(
        "mjc,jmcd->mjd", z_imag, w_real, precision=highest
    )
    b_real = jnp.einsum("mjd,zm->zjd", m_real, cos_z, precision=highest) - jnp.einsum(
        "mjd,zm->zjd", m_imag, sin_z, precision=highest
    )
    b_imag = jnp.einsum("mjd,zm->zjd", m_real, sin_z, precision=highest) + jnp.einsum(
        "mjd,zm->zjd", m_imag, cos_z, precision=highest
    )
    inverse_z = jnp.stack([b_real, b_imag], axis=2).reshape(grid_len, pair_count, 2 * chans)
    returned = lax.all_to_all(
        inverse_z.reshape(grid_len, 1, pair_count, 2 * chans),
        "slab",
        split_axis=0,
        concat_axis=1,
        tiled=True,
    )
    returned = returned.reshape(z_slab, n_slab, 1, pair_count, 2 * chans)
    gathered = lax.all_gather(returned, "pencil", axis=2, tiled=True)
    modes_all = gathered.reshape(z_slab, n_modes, n_modes, 2, chans)
    e_real = modes_all[:, :, :, 0]
    e_imag = modes_all[:, :, :, 1]
    r_real = jnp.einsum("zjkc,yj->zykc", e_real, cos_y, precision=highest) - jnp.einsum(
        "zjkc,yj->zykc", e_imag, sin_y, precision=highest
    )
    r_imag = jnp.einsum("zjkc,yj->zykc", e_real, sin_y, precision=highest) + jnp.einsum(
        "zjkc,yj->zykc", e_imag, cos_y, precision=highest
    )
    spectral = jnp.einsum("zykc,xk->zycx", r_real, cos_x, precision=highest) - jnp.einsum(
        "zykc,xk->zycx", r_imag, sin_x, precision=highest
    )
    spectral = spectral / float(grid_len * grid_len * grid_len)
    skipped = jnp.einsum("zycx,cd->zydx", field, skip.astype(jnp.float32), precision=highest)
    return jax.nn.gelu(spectral + skipped, approximate=True)


def per_device(point_feats, point_x, neighbour_dev, neighbour_line, spec_weight, skip_weight):
    n_slab = lax.axis_size("slab")
    n_pencil = lax.axis_size("pencil")
    n_devices = n_slab * n_pencil
    n_blocks, fanout = neighbour_dev.shape
    chans = point_feats.shape[1]
    block_len = point_feats.shape[0] // n_blocks
    grid_len = G
    z_slab = grid_len // n_slab
    y_rows = grid_len // n_pencil
    line_count = z_slab * y_rows
    capacity = max(2, 2 * n_blocks * fanout // n_devices)
    n_slots = n_devices * capacity
    features = point_feats.reshape(n_blocks, block_len, chans)
    coords = point_x.reshape(n_blocks, block_len)
    kernel = kernel_rows(coords, grid_len)
    target = neighbour_dev.reshape(-1)
    target_line = neighbour_line.reshape(-1)
    block_of = jnp.arange(n_blocks * fanout, dtype=jnp.int32) // fanout
    one_hot = (target[:, None] == jnp.arange(n_devices, dtype=jnp.int32)[None, :]).astype(jnp.int32)
    earlier = jnp.cumsum(one_hot, axis=0) - one_hot
    place_in = jnp.sum(earlier * one_hot, axis=1)
    slot_index = target * capacity + place_in
    slot_lines = jnp.full((n_slots,), -1, jnp.int32).at[slot_index].set(target_line)
    message = jnp.einsum(
        "bpc,bpx->bcx", features, kernel, preferred_element_type=jnp.float32
    ).astype(jnp.bfloat16)
    outgoing = (
        jnp.zeros((n_slots, chans, grid_len), jnp.bfloat16).at[slot_index].set(message[block_of])
    )
    arrived, arrived_lines = (
        lax.all_to_all(
            outgoing.reshape(n_devices, capacity, chans, grid_len),
            ("slab", "pencil"),
            split_axis=0,
            concat_axis=0,
            tiled=True,
        ),
        lax.all_to_all(
            slot_lines.reshape(n_devices, capacity),
            ("slab", "pencil"),
            split_axis=0,
            concat_axis=0,
            tiled=True,
        ),
    )
    arrived_msg = arrived.reshape(n_slots, chans * grid_len)
    picker = (
        jnp.arange(line_count, dtype=jnp.int32)[:, None] == arrived_lines.reshape(-1)[None, :]
    ).astype(jnp.bfloat16)
    grid_lines = jnp.dot(picker, arrived_msg, preferred_element_type=jnp.float32)
    field = grid_lines.reshape(z_slab, y_rows, chans, grid_len)
    for layer_index in range(spec_weight.shape[0]):
        field = spectral_layer(field, spec_weight[layer_index], skip_weight[layer_index])
    final_grid = field.astype(jnp.bfloat16).reshape(line_count, chans * grid_len)
    replies = jnp.dot(picker.T, final_grid, preferred_element_type=jnp.float32).astype(jnp.bfloat16)
    returned = lax.all_to_all(
        replies.reshape(n_devices, capacity, chans, grid_len),
        ("slab", "pencil"),
        split_axis=0,
        concat_axis=0,
        tiled=True,
    )
    values = returned.reshape(n_slots, chans, grid_len)[slot_index]
    pair_terms = dec_scale * jnp.einsum(
        "qpx,qcx->qpc", kernel[block_of], values, preferred_element_type=jnp.float32
    )
    summed = jnp.sum(pair_terms.reshape(n_blocks, fanout, block_len, chans), axis=1)
    return summed.reshape(n_blocks * block_len, chans)


def solution(mesh):
    in_specs = (
        P(("slab", "pencil"), None),
        P(("slab", "pencil")),
        P(("slab", "pencil"), None),
        P(("slab", "pencil"), None),
        P(None, ("slab", "pencil"), None, None, None, None),
        P(),
    )
    out_specs = P(("slab", "pencil"), None)
    return jax.shard_map(
        per_device, mesh=mesh, in_specs=in_specs, out_specs=out_specs, check_vma=False
    )
```

profile of v0, /device:TPU:1, one launch (start us, length us, event | category | flops | bytes accessed | tf_op | source)
XLA Modules:
  0.0 569.0 jit_solution(11706032376864767507)
XLA Ops:
  11.4 11.5 %all-to-all-start = ((s32[128,1,2]{2,1,0:T(1,128)}), s32[128,1,2]{2,1,0:T(1,128)S(1)}, u32[]{:S(2)}, u32[]{:S(2)}) async-start(s32[128,1,2]{2,1,0:T(1,128)} %bitcast.4), calls=%async_computation | async-start | bytes 131072 | tf_op jit(solution)/shard_map/all_to_all | solution.py:137
  28.8 15.7 %scatter_fusion = bf16[256,64,128]{2,1,0:T(8,128)(2,1)} fusion(bf16[256,64,128]{2,1,0:T(8,128)(2,1)} %broadcast_in_dim.5, s32[128]{0:T(128)S(1)} %fusion.236, bf16[128,64,128]{2,1,0:T(8,128)(2,1)S(1)} %gather_fusion.1), kind=kCustom, calls=%fused_computation.4 | custom fusion | bytes 6291968 | tf_op jit(solution)/shard_map/scatter | solution.py:127
  44.5 10.2 %all-to-all-start.1 = ((bf16[128,2,64,128]{3,2,1,0:T(8,128)(2,1)}), bf16[128,2,64,128]{3,2,1,0:T(8,128)(2,1)}, u32[]{:S(2)}, u32[]{:S(2)}) async-start(bf16[128,2,64,128]{3,2,1,0:T(8,128)(2,1)} %bitcast.332), calls=%async_computation.1 | async-start | bytes 8388608 | tf_op jit(solution)/shard_map/all_to_all | solution.py:130
  57.3 50.0 %all-to-all-done.1 = bf16[128,2,64,128]{3,2,1,0:T(8,128)(2,1)} async-done(((bf16[128,2,64,128]{3,2,1,0:T(8,128)(2,1)}), bf16[128,2,64,128]{3,2,1,0:T(8,128)(2,1)}, u32[]{:S(2)}, u32[]{:S(2)}) %all-to-all-start.1) | async-done | bytes 4194336 | tf_op jit(solution)/shard_map/all_to_all | solution.py:130
  107.3 12.3 %copy.347 = bf16[32,8,64,128]{3,1,2,0:T(8,128)(2,1)} copy(bf16[32,8,64,128]{3,2,1,0:T(8,128)(2,1)} %bitcast.114) | data formatting | bytes 8388608
  119.6 6.5 %copy.142 = bf16[8192,256]{1,0:T(8,128)(2,1)} copy(bf16[8192,256]{0,1:T(8,128)(2,1)} %bitcast.334) | data formatting | bytes 8388608 | tf_op jit(solution)/shard_map/dot_general | solution.py:149
  126.2 3.7 fusion.115
  129.9 12.7 %fusion.146 = f32[2,64,64,32]{1,3,2,0:T(8,128)} fusion(f32[2,64,64,128]{3,1,2,0:T(8,128)S(1)} %fusion.115, s32[32]{0:T(128)S(1)} %iota_add_fusion), kind=kOutput, calls=%fused_computation.185 | convolution fusion | flops 402710528 | bytes 5243008 | tf_op jit(solution)/shard_map/zycx,xk->zyck/dot_general | solution.py:36
  142.6 12.5 %fusion.60 = f32[2,64,64,32]{2,3,1,0:T(8,128)S(1)} fusion(f32[2,64,64,128]{3,1,2,0:T(8,128)S(1)} %fusion.115, s32[32]{0:T(128)S(1)} %iota_add_fusion), kind=kOutput, calls=%fused_computation.86 | convolution fusion | flops 402972672 | bytes 5243008 | tf_op jit(solution)/shard_map/zycx,xk->zyck/dot_general | solution.py:37
  171.6 14.9 %slice_bitcast_fusion.1 = (bf16[8,32,2,64,64]{4,3,2,1,0:T(8,128)(2,1)}, bf16[8,32,2,64,64]{4,3,2,1,0:T(8,128)(2,1)}) fusion(bf16[2,8,32,2,64,64]{5,4,3,2,1,0:T(8,128)(2,1)} %param.10), kind=kLoop, calls=%fused_computation.7 | loop fusion | bytes 16777216 | tf_op jit(solution)/shard_map/squeeze | solution.py:152
  186.5 7.1 %all-reduce.5.cloned.1.call-done = f32[2,64,2,8,128]{4,3,2,1,0:T(8,128)} async-done(((f32[2,64,2,8,128]{4,3,2,1,0:T(8,128)}), f32[2,64,2,8,128]{4,3,2,1,0:T(8,128)}) %all-reduce.5.cloned.1.call-update) | async-done | bytes 1048592
  196.1 10.1 %all-to-all-start.2 = ((f32[2,64,1,8,128]{4,3,2,0,1:T(8,128)}), f32[2,64,1,8,128]{4,3,2,0,1:T(8,128)S(1)}, u32[]{:S(2)}, u32[]{:S(2)}) async-start(f32[2,64,1,8,128]{4,3,2,0,1:T(8,128)} %copy.150), calls=%async_computation.2 | async-start | bytes 1048576 | tf_op jit(solution)/shard_map/all_to_all | solution.py:47
  206.2 12.2 %slice_bitcast_fusion.3 = (bf16[8,32,64,64]{3,2,1,0:T(8,128)(2,1)}, bf16[8,32,64,64]{3,2,1,0:T(8,128)(2,1)}, bf16[8,32,64,64]{3,2,1,0:T(8,128)(2,1)}, bf16[8,32,64,64]{3,2,1,0:T(8,128)(2,1)}) fusion(bf16[8,32,2,64,64]{4,3,2,1,0:T(8,128)(2,1)} %get-tuple-element.6, bf16[8,32,2,64,64]{4,3,2,1,0:T(8,128)(2,1)} %get-tuple-element.5), kind=kLoop, calls=%fused_computation.27 | loop fusion | bytes 16777216 | tf_op jit(solution)/shard_map/squeeze | solution.py:58
  224.3 5.3 fusion.29
  236.4 3.4 fusion.27
  243.1 21.2 %all_to_all.79 = f32[128,1,8,128]{3,2,1,0:T(8,128)S(1)} all-to-all(f32[128,1,8,128]{3,2,1,0:T(8,128)S(1)} %copy.154), channel_id=1, replica_groups=mesh['slab'=64,'pencil'=2] {'slab'}, dimensions={0} | all-to-all | bytes 1048576 | tf_op jit(solution)/shard_map/all_to_all | solution.py:73
  265.3 8.8 %fusion.15 = f32[2,64,128,64]{2,3,1,0:T(8,128)} fusion(f32[2,64,64,128]{3,1,2,0:T(8,128)} %copy-done.4, bf16[2,64,64]{2,1,0:T(8,128)(2,1)S(1)} %copy-done.11), kind=kOutput, calls=%fused_computation.33 | convolution fusion | flops 805306368 | bytes 8404992 | tf_op jit(solution)/shard_map/zycx,cd->zydx/dot_general | solution.py:95
  289.1 7.9 %fusion.46 = f32[2,64,64,128]{3,2,1,0:T(8,128)S(1)} fusion(f32[2,64,32,64]{3,1,2,0:T(8,128)S(1)} %subtract_bitcast_fusion.1, s32[32]{0:T(128)S(1)} %iota_add_fusion), kind=kOutput, calls=%fused_computation.68 | convolution fusion | flops 402710528 | bytes 5243008 | tf_op jit(solution)/shard_map/zykc,xk->zycx/dot_general | solution.py:91
  299.6 9.1 %fusion.6 = f32[2,64,64,128]{3,2,1,0:T(8,128)S(1)} fusion(f32[2,64,128,64]{2,3,1,0:T(8,128)S(1)} %copy-done.6, f32[2,64,64,128]{3,2,1,0:T(8,128)S(1)} %fusion.46, f32[2,64,32,64]{3,1,2,0:T(8,128)S(1)} %add_bitcast_fusion.1, s32[32]{0:T(128)S(1)} %iota_add_fusion), kind=kOutput, calls=%fused_computation.16 | convolution fusion | flops 414244864 | bytes 13631616 | tf_op jit(solution)/shard_map/zykc,xk->zycx/dot_general | solution.py:91
  308.7 11.6 %convolution_negate_fusion = f32[2,64,64,32]{2,3,1,0:T(8,128)S(1)} fusion(f32[2,64,64,128]{3,2,1,0:T(8,128)S(1)} %fusion.6, s32[32]{0:T(128)S(1)} %iota_add_fusion), kind=kOutput, calls=%fused_computation.87 | convolution fusion | flops 402972672 | bytes 5243008 | tf_op jit(solution)/shard_map/zycx,xk->zyck/dot_general | solution.py:37
  320.2 11.5 %fusion.143 = f32[2,64,64,32]{2,3,1,0:T(8,128)S(1)} fusion(f32[2,64,64,128]{3,2,1,0:T(8,128)S(1)} %fusion.6, s32[32]{0:T(128)S(1)} %iota_add_fusion), kind=kOutput, calls=%fused_computation.182 | convolution fusion | flops 402710528 | bytes 5243008 | tf_op jit(solution)/shard_map/zycx,xk->zyck/dot_general | solution.py:36
  346.0 26.6 %all-reduce.7.cloned.1.call-done = f32[2,64,2,8,128]{4,3,2,1,0:T(8,128)} async-done(((f32[2,64,2,8,128]{4,3,2,1,0:T(8,128)}), f32[2,64,2,8,128]{4,3,2,1,0:T(8,128)}) %all-reduce.7.cloned.1.call-update) | async-done | bytes 1048592
  374.3 22.3 %all_to_all.80 = f32[2,64,1,8,128]{4,3,2,0,1:T(8,128)S(1)} all-to-all(f32[2,64,1,8,128]{4,3,2,0,1:T(8,128)S(1)} %copy.168), channel_id=1, replica_groups=mesh['slab'=64,'pencil'=2] {'slab'}, dimensions={1} | all-to-all | bytes 1048576 | tf_op jit(solution)/shard_map/all_to_all | solution.py:47
  402.3 5.6 fusion.21
  421.2 15.6 %all_to_all.81 = f32[128,1,8,128]{3,2,1,0:T(8,128)S(1)} all-to-all(f32[128,1,8,128]{3,2,1,0:T(8,128)S(1)} %copy.172), channel_id=1, replica_groups=mesh['slab'=64,'pencil'=2] {'slab'}, dimensions={0} | all-to-all | bytes 1048576 | tf_op jit(solution)/shard_map/all_to_all | solution.py:73
  437.7 10.5 %all-gather.5.cloned.1.call-done = f32[2,64,2,8,128]{4,3,1,0,2:T(8,128)} async-done(((f32[2,64,1,8,128]{4,3,1,0,2:T(8,128)}), f32[2,64,2,8,128]{4,3,1,0,2:T(8,128)}) %all-gather.5.cloned.1.call-update) | async-done | bytes 1048592 | tf_op jit(solution)/shard_map/all_gather | solution.py:81
  462.9 8.1 %fusion.43 = f32[2,64,64,128]{3,2,1,0:T(8,128)S(1)} fusion(f32[2,64,32,64]{3,1,2,0:T(8,128)S(1)} %subtract_bitcast_fusion, s32[32]{0:T(128)S(1)} %iota_add_fusion), kind=kOutput, calls=%fused_computation.65 | convolution fusion | flops 402710528 | bytes 5243008 | tf_op jit(solution)/shard_map/zykc,xk->zycx/dot_general | solution.py:91
  473.5 7.9 %fusion.41 = f32[2,64,64,128]{3,2,1,0:T(8,128)S(1)} fusion(f32[2,64,32,64]{3,1,2,0:T(8,128)S(1)} %add_bitcast_fusion, s32[32]{0:T(128)S(1)} %iota_add_fusion), kind=kOutput, calls=%fused_computation.63 | convolution fusion | flops 402710528 | bytes 5243008 | tf_op jit(solution)/shard_map/zykc,xk->zycx/dot_general | solution.py:91
  481.4 4.2 fusion.14
  490.5 9.6 %all-to-all-start.6 = ((bf16[128,2,64,128]{3,2,1,0:T(8,128)(2,1)}), bf16[128,2,64,128]{3,2,1,0:T(8,128)(2,1)}, u32[]{:S(2)}, u32[]{:S(2)}) async-start(bf16[128,2,64,128]{3,2,1,0:T(8,128)(2,1)} %bitcast.333), calls=%async_computation.6 | async-start | bytes 8388608 | tf_op jit(solution)/shard_map/all_to_all | solution.py:155
  504.0 48.8 %all-to-all-done.6 = bf16[128,2,64,128]{3,2,1,0:T(8,128)(2,1)} async-done(((bf16[128,2,64,128]{3,2,1,0:T(8,128)(2,1)}), bf16[128,2,64,128]{3,2,1,0:T(8,128)(2,1)}, u32[]{:S(2)}, u32[]{:S(2)}) %all-to-all-start.6) | async-done | bytes 4194336 | tf_op jit(solution)/shard_map/all_to_all | solution.py:155
  556.0 5.3 bitcast_reduce_fusion
  (140 shorter events, 132.2 us)
Async XLA Ops:
  6.5 17.1 %copy-start = (bf16[4096,64]{0,1:T(8,128)(2,1)S(1)}, bf16[4096,64]{0,1:T(8,128)(2,1)}, u32[]{:S(2)}) copy-start(bf16[4096,64]{0,1:T(8,128)(2,1)} %param.6) | copy-start | bytes 1572868
  11.4 33.1 %all-to-all-start = ((s32[128,1,2]{2,1,0:T(1,128)}), s32[128,1,2]{2,1,0:T(1,128)S(1)}, u32[]{:S(2)}, u32[]{:S(2)}) async-start(s32[128,1,2]{2,1,0:T(1,128)} %bitcast.4), calls=%async_computation | async-start | bytes 131072 | tf_op jit(solution)/shard_map/all_to_all | solution.py:137
  44.5 10.7 %copy-start.12 = (u32[128]{0:T(128)S(1)}, u32[128]{0:T(128)}, u32[]{:S(2)}) copy-start(u32[128]{0:T(128)} %constant.104) | copy-start | bytes 1540
  44.5 62.8 %all-to-all-start.1 = ((bf16[128,2,64,128]{3,2,1,0:T(8,128)(2,1)}), bf16[128,2,64,128]{3,2,1,0:T(8,128)(2,1)}, u32[]{:S(2)}, u32[]{:S(2)}) async-start(bf16[128,2,64,128]{3,2,1,0:T(8,128)(2,1)} %bitcast.332), calls=%async_computation.1 | async-start | bytes 8388608 | tf_op jit(solution)/shard_map/all_to_all | solution.py:130
  54.7 138.9 %all-reduce.5.cloned.1.call-start = ((), (), s32[]{:S(2)}) async-start(), calls=%async_computation.9 | async-start | bytes 2097152
  129.8 12.7 %copy-start.4 = (f32[2,64,64,128]{3,1,2,0:T(8,128)}, f32[2,64,64,128]{3,1,2,0:T(8,128)S(1)}, u32[]{:S(2)}) copy-start(f32[2,64,64,128]{3,1,2,0:T(8,128)S(1)} %fusion.115) | copy-start | bytes 12582916
  158.4 3.0 copy-start.5
  196.1 22.5 %all-to-all-start.2 = ((f32[2,64,1,8,128]{4,3,2,0,1:T(8,128)}), f32[2,64,1,8,128]{4,3,2,0,1:T(8,128)S(1)}, u32[]{:S(2)}, u32[]{:S(2)}) async-start(f32[2,64,1,8,128]{4,3,2,0,1:T(8,128)} %copy.150), calls=%async_computation.2 | async-start | bytes 1048576 | tf_op jit(solution)/shard_map/all_to_all | solution.py:47
  206.2 68.8 %all-gather.3.cloned.1.call-start = ((), (), s32[]{:S(2)}) async-start(), calls=%async_computation.7 | async-start | bytes 1572864 | tf_op jit(solution)/shard_map/all_gather | solution.py:81
  221.6 8.0 %copy-start.10 = (bf16[8,32,64,64]{3,2,1,0:T(8,128)(2,1)S(1)}, bf16[8,32,64,64]{3,2,1,0:T(8,128)(2,1)}, u32[]{:S(2)}) copy-start(bf16[8,32,64,64]{3,2,1,0:T(8,128)(2,1)} %get-tuple-element.20) | copy-start | bytes 6291460
  229.6 6.7 %copy-start.9 = (bf16[8,32,64,64]{3,2,1,0:T(8,128)(2,1)S(1)}, bf16[8,32,64,64]{3,2,1,0:T(8,128)(2,1)}, u32[]{:S(2)}) copy-start(bf16[8,32,64,64]{3,2,1,0:T(8,128)(2,1)} %get-tuple-element.19) | copy-start | bytes 6291460
  239.7 25.5 %copy-start.11 = (bf16[2,64,64]{2,1,0:T(8,128)(2,1)S(1)}, bf16[2,64,64]{2,1,0:T(8,128)(2,1)}, u32[]{:S(2)}) copy-start(bf16[2,64,64]{2,1,0:T(8,128)(2,1)} %param.11) | copy-start | bytes 49156
  265.2 107.4 %all-reduce.7.cloned.1.call-start = ((), (), s32[]{:S(2)}) async-start(), calls=%async_computation.10 | async-start | bytes 2097152
  297.0 2.6 copy-start.6
  308.7 23.1 %copy-start.2 = (f32[2,64,64,128]{3,2,1,0:T(8,128)}, f32[2,64,64,128]{3,2,1,0:T(8,128)S(1)}, u32[]{:S(2)}) copy-start(f32[2,64,64,128]{3,2,1,0:T(8,128)S(1)} %fusion.6) | copy-start | bytes 12582916
  346.0 102.2 %all-gather.5.cloned.1.call-start = ((), (), s32[]{:S(2)}) async-start(), calls=%async_computation.8 | async-start | bytes 1572864 | tf_op jit(solution)/shard_map/all_gather | solution.py:81
  399.7 8.3 %copy-start.8 = (bf16[8,32,64,64]{3,2,1,0:T(8,128)(2,1)S(1)}, bf16[8,32,64,64]{3,2,1,0:T(8,128)(2,1)}, u32[]{:S(2)}) copy-start(bf16[8,32,64,64]{3,2,1,0:T(8,128)(2,1)} %get-tuple-element.7) | copy-start | bytes 6291460
  407.9 6.7 %copy-start.7 = (bf16[8,32,64,64]{3,2,1,0:T(8,128)(2,1)S(1)}, bf16[8,32,64,64]{3,2,1,0:T(8,128)(2,1)}, u32[]{:S(2)}) copy-start(bf16[8,32,64,64]{3,2,1,0:T(8,128)(2,1)} %get-tuple-element.8) | copy-start | bytes 6291460
  473.5 7.9 %copy-start.3 = (f32[2,64,64,128]{3,2,1,0:T(8,128)S(1)}, f32[2,64,64,128]{3,2,1,0:T(8,128)}, u32[]{:S(2)}) copy-start(f32[2,64,64,128]{3,2,1,0:T(8,128)} %copy-done.2) | copy-start | bytes 12582916
  490.5 62.3 %all-to-all-start.6 = ((bf16[128,2,64,128]{3,2,1,0:T(8,128)(2,1)}), bf16[128,2,64,128]{3,2,1,0:T(8,128)(2,1)}, u32[]{:S(2)}, u32[]{:S(2)}) async-start(bf16[128,2,64,128]{3,2,1,0:T(8,128)(2,1)} %bitcast.333), calls=%async_computation.6 | async-start | bytes 8388608 | tf_op jit(solution)/shard_map/all_to_all | solution.py:155
  552.8 9.5 %copy-start.1 = (bf16[4096,64]{0,1:T(8,128)(2,1)S(1)}, bf16[4096,64]{0,1:T(8,128)(2,1)}, u32[]{:S(2)}) copy-start(bf16[4096,64]{0,1:T(8,128)(2,1)} %param.6) | copy-start | bytes 1572868
Sparse Core Ops, SparseCore 0:
  171.7 21.8 all-reduce.4
  265.3 9.6 all-gather.2
  346.1 26.4 all-reduce.6
  437.8 10.3 all-gather.4
where the time goes:
time: 574 us; the launch traced here: 569 us
  matrix products  189 us (33%)
  waiting for transfers between devices  144 us (25%)
  local copies, waits for them, and re-layouts  117 us (20%)
  blocking collectives  59.2 us (10%)
  starting transfers between devices  42.1 us (7%)
  between operations  14.1 us (2%)
    all_to_all x1, waiting for transfers between devices, per_device(): lax.all_to_all(outgoing.reshape(n_devices, capacity, chans, grid_len), ('...  50 us
    all_to_all x1, waiting for transfers between devices, per_device(): lax.all_to_all(replies.reshape(n_devices, capacity, chans, grid_len), ('s...  48.8 us
    all_to_all x2, blocking collectives, spectral_layer(): lax.all_to_all(inverse_z.reshape(grid_len, 1, pair_count, 2 * chans), 'sl...  36.8 us
    unnamed x6, waiting for transfers between devices  33.8 us
    dot_general x2, matrix products, spectral_layer(): x_real = jnp.einsum('zycx,xk->zyck', field, cos_x, precision=highest)  24.2 us
    dot_general x2, matrix products, spectral_layer(): x_imag = -jnp.einsum('zycx,xk->zyck', field, sin_x, precision=highest)  24.1 us
    all_to_all x1, blocking collectives, spectral_layer(): lax.all_to_all(summed, 'slab', split_axis=1, concat_axis=0, tiled=True)  22.3 us
    unnamed x37, local copies, waits for them, and re-layouts  22.3 us
  transfers between devices with their start and end apart: 8, of which 7 were waited for; matrix products, arithmetic and copies ran while one was open for 11% of the time, Pallas kernels for 0%

commit v1 on v0

v1 whole, which is shorter than its diff:
```python
import functools

import jax
import jax.numpy as jnp
import numpy as np
from jax import lax
from jax.experimental import pallas as pl
from jax.experimental.pallas import tpu as pltpu
from jax.sharding import PartitionSpec as P

G = 128
C = 64
M = 32
NDEV = 128
MESH = pl.DeviceIdType.MESH
BF = jnp.bfloat16
F32 = jnp.float32
VLIM = 60 * 1024 * 1024


def trig(cells):
    waves = np.arange(M) - M // 2
    ang = ((cells[:, None] * waves[None, :]) % G) * (2.0 * np.pi / G)
    return np.cos(ang), np.sin(ang)


def split_np(t):
    hi = np.asarray(t, np.float32).astype(jnp.bfloat16)
    lo = (np.asarray(t, np.float64) - hi.astype(np.float64)).astype(np.float32).astype(jnp.bfloat16)
    return hi, lo


def tall(t):
    hi, lo = split_np(t)
    return np.concatenate([np.concatenate([hi, hi], 1), np.concatenate([lo, np.zeros_like(lo)], 1)], 0)


def wide(t):
    hi, lo = split_np(t)
    return np.concatenate([hi, hi, lo], 1)


def make_tables():
    cos, sin = trig(np.arange(G))
    yf = tall(np.concatenate([cos.T, -sin.T], 0))
    zf = []
    for z1 in range(2):
        c, s = trig(2 * np.arange(G // 2) + z1)
        zf.append(tall(np.concatenate([np.concatenate([c.T, s.T], 1), np.concatenate([-s.T, c.T], 1)], 0)))
    zf = np.concatenate(zf, 0)
    xf = tall(np.concatenate([cos.T, sin.T], 0))
    xi = wide(np.concatenate([cos, sin], 1) / float(G) ** 3)
    zi = wide(np.concatenate([np.concatenate(trig(2 * np.arange(G // 2) + z1), 1) for z1 in range(2)], 0))
    yi = wide(np.concatenate([cos, -sin], 1))
    return yf, zf, xf, xi, zi, yi


def split2(v):
    hi = v.astype(BF)
    return hi, (v - hi.astype(F32)).astype(BF)


def dot(a, b):
    return jnp.dot(a, b, preferred_element_type=F32)


def lane_lo(shape):
    return lax.broadcasted_iota(jnp.int32, shape, 1) < C


def swap(v):
    return pltpu.roll(v, C, 1)


def y_forward(yf, plane, a_ref, slab):
    hi, lo = split2(plane)
    out = dot(yf, jnp.concatenate([hi, lo], 0))
    out = out[:2 * M] + out[2 * M:]
    a_ref[pl.ds(slab, M, stride=G), :] = out[:M]
    a_ref[pl.ds(slab + 64, M, stride=G), :] = out[M:]


def z_forward(zf, a_ref, ky):
    hi, lo = split2(a_ref[pl.ds(pl.multiple_of(ky * G, G), G), :])
    out = dot(zf, jnp.concatenate([hi, lo], 0))
    o0 = out[:64] + out[64:128]
    o1 = out[128:192] + out[192:]
    low = lane_lo((M, G))
    main = jnp.where(low, o0[:M], o1[M:])
    other = jnp.where(low, o0[M:], o1[:M])
    return main + swap(other)


def x_forward(xf, plane):
    hi, lo = split2(plane)
    out = dot(xf, jnp.concatenate([hi, lo], 0))
    out = out[:64] + out[64:]
    rot = swap(out[M:])
    return out[:M] + jnp.where(lane_lo((M, G)), rot, -rot)


def stack3(rows):
    hi, lo = split2(rows)
    return jnp.concatenate([hi, lo, hi], 0)


def mode_inverse(table, modes):
    rot = swap(modes)
    rot = jnp.where(lane_lo((M, G)), -rot, rot)
    return dot(table, stack3(jnp.concatenate([modes, rot], 0)))


def z_inverse(zi, modes, iz_ref, ky):
    out = mode_inverse(zi, modes)
    o0, o1 = out[:64], out[64:]
    low = lane_lo((64, G))
    iz_ref[pl.ds(ky, 64, stride=64), :] = jnp.where(low, o0, swap(o1))
    iz_ref[pl.ds(ky + M, 64, stride=64), :] = jnp.where(low, swap(o0), o1)


def gelu(v):
    k = 0.7978845608028654
    return 0.5 * v * (1.0 + jnp.tanh(k * (v + 0.044715 * (v * v * v))))


def y_inverse_act(yi, skip2, iz_ref, plane, slab):
    rows = iz_ref[pl.ds(pl.multiple_of(slab * 64, 64), 64), :]
    hi, lo = split2(plane)
    spectral = dot(yi, stack3(rows))
    skipped = dot(jnp.concatenate([hi, lo], 1), skip2)
    return gelu(spectral + skipped)


def unpack_messages(r_ref, msg_ref):
    def body(sg, _):
        v = r_ref[pl.ds(sg * 8, 8)].reshape(G, G).astype(F32)
        w = swap(v)
        low = lane_lo((G, G))
        msg_ref[sg, :G, :] = jnp.where(low, v, w).astype(BF)
        msg_ref[sg, G:, :] = jnp.where(low, w, v).astype(BF)
        return 0
    lax.fori_loop(0, 16, body, 0)


def expand(msg_ref, ie_ref, rows_ref):
    def body(sg, _):
        idx = ie_ref[sg]
        msg = msg_ref[sg]
        lanes = lax.broadcasted_iota(jnp.int32, (16, 256), 1)
        for og in range(16):
            hot = [jnp.where(idx[:, o:o + 1] == lanes, 1.0, 0.0).astype(BF) for o in range(og * 8, og * 8 + 8)]
            out = dot(jnp.concatenate(hot, 0), msg).astype(BF)
            rows_ref[og * 8:og * 8 + 8, pl.ds(pl.multiple_of(sg * 16, 16), 16), :] = out.reshape(8, 16, G)
        return 0
    lax.fori_loop(0, 16, body, 0)


def scatter_lines(rows_ref, lt_ref, o):
    lines = lax.broadcasted_iota(jnp.int32, (G, 256), 0)
    hot = jnp.where(lt_ref[o] == lines, 1.0, 0.0).astype(BF)
    out = dot(hot, rows_ref[o])
    return jnp.where(lane_lo((64, G)), out[:64], out[64:])


def gather_lines(half, ls, j):
    low = lane_lo((64, G))
    rhs = jnp.concatenate([jnp.where(low, half, 0.0), jnp.where(low, 0.0, half)], 0).astype(BF)
    lanes = lax.broadcasted_iota(jnp.int32, (256, G), 1)
    hot = jnp.where(ls[:, j:j + 1] == lanes, 1.0, 0.0).astype(BF)
    return dot(hot, rhs).astype(BF)


def block_sums(rows2_ref, iet_ref, out_ref):
    def body(sg, _):
        codes = iet_ref[sg]
        rows = lax.broadcasted_iota(jnp.int32, (256, 256), 0)
        acc = jnp.zeros((256, G), F32)
        for k in range(8):
            hot = jnp.where(codes[:, k * 256:(k + 1) * 256] == rows, 1.0, 0.0).astype(BF)
            acc = acc + dot(hot, rows2_ref[sg, k * 16:(k + 1) * 16].reshape(256, G))
        acc = acc + swap(acc)
        out = jnp.where(lane_lo((G, G)), acc[:G], acc[G:]).astype(BF)
        out_ref[pl.ds(sg * 8, 8)] = out.reshape(8, 16, G)
        return 0
    lax.fori_loop(0, 16, body, 0)


def mode_product(f8, w_ref, kz):
    low = lane_lo((8, G))
    a = jnp.where(low, f8, -f8)
    b = swap(f8)
    ah, al = split2(a)
    bh, bl = split2(b)
    lhs = jnp.concatenate([ah.astype(F32), al.astype(F32), bh.astype(F32), bl.astype(F32)], 0).astype(BF)
    row = lax.broadcasted_iota(jnp.int32, (8, C), 0)
    re = jnp.zeros((8, C), F32)
    im = jnp.zeros((8, C), F32)
    for j in range(8):
        out = dot(lhs, w_ref[j, kz])
        re = jnp.where(row == j, out[0:8] + out[8:16], re)
        im = jnp.where(row == j, out[16:24] + out[24:32], im)
    return jnp.concatenate([re, im], 1)


def encode_kernel(r_ref, ie_ref, lt_ref, yf_ref, zf_ref, field_ref, send_ref, msg_ref, rows_ref, a_ref):
    unpack_messages(r_ref, msg_ref)
    expand(msg_ref, ie_ref, rows_ref)

    def per_slab(slab, _):
        plane = jnp.concatenate([scatter_lines(rows_ref, lt_ref, 2 * slab), scatter_lines(rows_ref, lt_ref, 2 * slab + 1)], 0)
        field_ref[slab] = plane
        y_forward(yf_ref[...], plane, a_ref, slab)
        return 0
    lax.fori_loop(0, 64, per_slab, 0)
    forward_modes(zf_ref, a_ref, send_ref)


def forward_modes(zf_ref, a_ref, send_ref):
    def per_ky(ky, _):
        send_ref[pl.ds(ky * 4, 4)] = z_forward(zf_ref[...], a_ref, ky).reshape(4, 8, G)
        return 0
    lax.fori_loop(0, M, per_ky, 0)


def inverse_modes(rx_ref, zi_ref, iz_ref):
    def per_ky(ky, _):
        z_inverse(zi_ref[...], rx_ref[pl.ds(ky * 4, 4)].reshape(M, G), iz_ref, ky)
        return 0
    lax.fori_loop(0, M, per_ky, 0)


def middle_kernel(rx_ref, field_ref, skip2_ref, zi_ref, yi_ref, yf_ref, zf_ref, out_ref, send_ref, iz_ref, a_ref):
    inverse_modes(rx_ref, zi_ref, iz_ref)

    def per_slab(slab, _):
        plane = y_inverse_act(yi_ref[...], skip2_ref[...], iz_ref, field_ref[slab], slab)
        out_ref[slab] = plane
        y_forward(yf_ref[...], plane, a_ref, slab)
        return 0
    lax.fori_loop(0, 64, per_slab, 0)
    forward_modes(zf_ref, a_ref, send_ref)


def final_kernel(rx_ref, field_ref, skip2_ref, zi_ref, yi_ref, ls_ref, iet_ref, out_ref, iz_ref, rows2_ref):
    inverse_modes(rx_ref, zi_ref, iz_ref)

    def per_group(g, _):
        ls = ls_ref[g]
        for i in range(4):
            slab = g * 4 + i
            plane = y_inverse_act(yi_ref[...], skip2_ref[...], iz_ref, field_ref[slab], slab)
            for p in range(2):
                got = gather_lines(plane[64 * p:64 * p + 64], ls, 2 * i + p)
                rows2_ref[:, 2 * slab + p, :, :] = got.reshape(16, 16, G)
        return 0
    lax.fori_loop(0, 16, per_group, 0)
    block_sums(rows2_ref, iet_ref, out_ref)


def spectrum_kernel(rx_ref, w_ref, xf_ref, xi_ref, out_ref, gs_ref, gr_ref, hs_ref, hr_ref, sems):
    slab = lax.axis_index("slab")
    pencil = lax.axis_index("pencil")
    q = lax.rem(slab, 2) * 2 + pencil
    base = slab - lax.rem(slab, 2)

    def peer(i):
        other = lax.rem(q + i, 4)
        return other, (base + lax.div(other, 2), lax.rem(other, 2))

    barrier = pltpu.get_barrier_semaphore()
    for i in range(1, 4):
        pl.semaphore_signal(barrier, inc=1, device_id=peer(i)[1], device_id_type=MESH)

    rows = rx_ref.shape[0]

    def fwd(kz, _):
        plane = rx_ref[pl.ds(kz, G, stride=8), :]
        gs_ref[:, kz] = x_forward(xf_ref[...], plane).reshape(4, 8, G)
        return 0
    lax.fori_loop(0, 8, fwd, 0)

    def exchange(src, dst, st):
        local = pltpu.make_async_copy(src.at[q], dst.at[q], sems.at[st, 2])
        local.start()
        if st == 0:
            pl.semaphore_wait(barrier, 3)
        for i in range(1, 4):
            other, did = peer(i)
            pltpu.make_async_remote_copy(src.at[other], dst.at[q], sems.at[st, 0], sems.at[st, 1], device_id=did, device_id_type=MESH).start()
        local.wait()
        three = pl.ds(0, 3)
        pltpu.make_async_copy(src.at[three], src.at[three], sems.at[st, 0]).wait()
        pltpu.make_async_copy(dst.at[three], dst.at[three], sems.at[st, 1]).wait()

    exchange(gs_ref, gr_ref, 0)

    def modes(kz, _):
        g, k = lax.div(kz, 8), lax.rem(kz, 8)
        hs_ref[g, k] = mode_product(gr_ref[g, k], w_ref, kz)
        return 0
    lax.fori_loop(0, M, modes, 0)
    exchange(hs_ref, hr_ref, 1)

    def inv(kz, _):
        out_ref[pl.ds(kz, G, stride=8), :] = mode_inverse(xi_ref[...], hr_ref[:, kz].reshape(M, G))
        return 0
    lax.fori_loop(0, 8, inv, 0)


def call(kernel, outs, args, scratch, name, **params):
    vm = pl.BlockSpec(memory_space=pltpu.VMEM)
    return pl.pallas_call(
        kernel,
        out_shape=[jax.ShapeDtypeStruct(s, d) for s, d in outs],
        in_specs=[vm] * len(args),
        out_specs=[vm] * len(outs),
        scratch_shapes=scratch,
        compiler_params=pltpu.CompilerParams(vmem_limit_bytes=VLIM, **params),
        name=name,
    )(*args)


def kernel_rows(coords):
    offset_x = coords[..., None] * G - jnp.arange(G, dtype=F32)
    return jnp.exp(-offset_x * offset_x / (2.0 * 0.5 * 0.5)).astype(BF)


def slot_tables(neighbour_dev, neighbour_line):
    nb, fan = neighbour_dev.shape
    dev = neighbour_dev.reshape(-1)
    code = (jnp.arange(nb * fan, dtype=jnp.int32) // fan) * G + neighbour_line.reshape(-1)
    hit = dev[:, None] == jnp.arange(NDEV, dtype=jnp.int32)[None, :]
    first = jnp.min(jnp.where(hit, code[:, None], nb * G), axis=0)
    last = jnp.max(jnp.where(hit, code[:, None], -1), axis=0)
    first = jnp.where(first == nb * G, -1, first)
    second = jnp.where(last == first, -1, last)
    return jnp.stack([first, second], 0)


def route_tables(codes):
    s8 = (jnp.arange(NDEV, dtype=jnp.int32) % 8)[:, None, None]
    block = codes // G
    kpos = jnp.where(codes >= 0, (block // 16) * 128 + s8 * 16 + block % 16, -1)
    line = jnp.where(codes >= 0, codes % G, -1)
    ie = kpos.reshape(16, 16, NDEV)
    iet = ie.transpose(0, 2, 1).reshape(16, 1, 2048)
    flat = line.reshape(256, NDEV)
    lt = flat.T.reshape(NDEV, 1, 256)
    ls = flat.reshape(256, 16, 8).transpose(1, 0, 2)
    return ie, iet, lt, ls


def all_to_all(v):
    return lax.all_to_all(v, ("slab", "pencil"), split_axis=0, concat_axis=0, tiled=True)


def per_device(point_feats, point_x, neighbour_dev, neighbour_line, spec_weight, skip_weight):
    yf, zf, xf, xi, zi, yi = [jnp.asarray(t) for t in make_tables()]
    nb = neighbour_dev.shape[0]
    feats = point_feats.reshape(nb, -1, C)
    kernel = kernel_rows(point_x.reshape(nb, -1))
    codes = lax.all_gather(slot_tables(neighbour_dev, neighbour_line), ("slab", "pencil"), axis=0)
    message = jnp.einsum("bpx,bpc->bxc", kernel, feats, preferred_element_type=F32).astype(BF)
    outgoing = message.reshape(2, 16, G, C).transpose(2, 1, 0, 3).reshape(G, 16, 2 * C)
    arrived = all_to_all(outgoing)
    ie, iet, lt, ls = route_tables(codes)
    zero = jnp.zeros((C, C), BF)
    sk = [jnp.block([[w, zero], [zero, w]]) for w in skip_weight]
    skip2 = [jnp.concatenate([s, s], 0) for s in sk]
    weights = spec_weight.reshape(2, 8, M, 2 * C, C)

    mode_shape = ((NDEV, 8, G), F32)
    field_shape = ((64, G, G), F32)
    field, send = call(
        encode_kernel, [field_shape, mode_shape], [arrived, ie, lt, yf, zf],
        [pltpu.VMEM((16, 256, G), BF), pltpu.VMEM((NDEV, 256, G), BF), pltpu.VMEM((M * G, G), F32)], "encode",
    )

    def spectrum(send, layer):
        rx = all_to_all(send).reshape(NDEV * 8, G)
        (back,) = call(
            spectrum_kernel, [((NDEV * 8, G), F32)], [rx, weights[layer], xf, xi],
            [pltpu.VMEM((4, 8, 8, G), F32)] * 4 + [pltpu.SemaphoreType.DMA((2, 3))], f"spectrum{layer}",
            collective_id=1 + layer, has_side_effects=True,
        )
        return all_to_all(back.reshape(NDEV, 8, G))

    back = spectrum(send, 0)
    field, send = call(
        middle_kernel, [field_shape, mode_shape], [back, field, skip2[0], zi, yi, yf, zf],
        [pltpu.VMEM((64 * 64, G), F32), pltpu.VMEM((M * G, G), F32)], "middle",
    )
    back = spectrum(send, 1)
    (sums,) = call(
        final_kernel, [((NDEV, 16, G), BF)], [back, field, skip2[1], zi, yi, ls, iet],
        [pltpu.VMEM((64 * 64, G), F32), pltpu.VMEM((16, NDEV, 16, G), BF)], "final",
    )
    values = all_to_all(sums)
    values = values.reshape(G, 16, 2, C).transpose(2, 1, 0, 3).reshape(nb, G, C)
    out = 0.5 * jnp.einsum("bpx,bxc->bpc", kernel, values, preferred_element_type=F32)
    return out.reshape(-1, C)


def solution(mesh):
    both = ("slab", "pencil")
    in_specs = (P(both, None), P(both), P(both, None), P(both, None), P(None, both, None, None, None, None), P())
    return jax.shard_map(per_device, mesh=mesh, in_specs=in_specs, out_specs=P(both, None), check_vma=False)
```

time: 574 us -> 340 us (0.59)
  matrix products: 189 us -> 2.22 us
  Pallas kernels: 0 us -> 181 us
  waiting for transfers between devices: 144 us -> 21.4 us
  local copies, waits for them, and re-layouts: 117 us -> 26.9 us
  blocking collectives: 59.2 us -> 75.2 us
  between operations: 14.1 us -> 0.21 us
  starting transfers between devices: 42.1 us -> 29.2 us
    dot_general x54 -> x2, matrix products: 189 us -> 2.22 us  [the longest x1 1.13 us: per_device(): jnp.einsum('bpx,bxc->bpc', kernel, values, preferred_element_type=F32)]
    pallas_call x0 -> x5, Pallas kernels: none -> 181 us  [call(): pl.pallas_call(kernel, out_shape=[jax.ShapeDtypeStruct(s, d) for s, d in...]
    all_to_all x4, waiting for transfers between devices: 99 us -> 21.4 us  [all_to_all(): lax.all_to_all(v, ('slab', 'pencil'), split_axis=0, concat_axis=0, tiled=...]
    all_gather x0 -> x1, blocking collectives: none -> 37.4 us  [per_device(): lax.all_gather(slot_tables(neighbour_dev, neighbour_line), ('slab', 'penc...]
    unnamed x6 -> x0, waiting for transfers between devices: 33.8 us -> none
    squeeze x2 -> x0, local copies, waits for them, and re-layouts: 27.1 us -> none  [the longest x1 14.9 us: per_device(): spec_weight[layer_index]]
    all_to_all x3 -> x2, blocking collectives: 59.2 us -> 37.8 us  [all_to_all(): lax.all_to_all(v, ('slab', 'pencil'), split_axis=0, concat_axis=0, tiled=...]
    unnamed x37 -> x20, local copies, waits for them, and re-layouts: 22.3 us -> 3.64 us
  transfers between devices with their start and end apart: 8 -> 4, of which waited for: 7 -> 2; matrix products, arithmetic and copies ran while one was open for 11% -> 7% of each run, Pallas kernels for 0% -> 0%
where the time goes in v1:
time: 340 us
  Pallas kernels  181 us (53%)
  blocking collectives  75.2 us (22%)
  starting transfers between devices  29.2 us (9%)
  local copies, waits for them, and re-layouts  26.9 us (8%)
  waiting for transfers between devices  21.4 us (6%)
  other arithmetic  3.81 us (1%)
    pallas_call x5, Pallas kernels, call(): pl.pallas_call(kernel, out_shape=[jax.ShapeDtypeStruct(s, d) for s, d in...  181 us
    all_to_all x2, blocking collectives, all_to_all(): lax.all_to_all(v, ('slab', 'pencil'), split_axis=0, concat_axis=0, tiled=...  37.8 us
    all_gather x1, blocking collectives, per_device(): lax.all_gather(slot_tables(neighbour_dev, neighbour_line), ('slab', 'penc...  37.4 us
    all_to_all x4, starting transfers between devices, all_to_all(): lax.all_to_all(v, ('slab', 'pencil'), split_axis=0, concat_axis=0, tiled=...  29.2 us
    all_to_all x4, waiting for transfers between devices, all_to_all(): lax.all_to_all(v, ('slab', 'pencil'), split_axis=0, concat_axis=0, tiled=...  21.4 us
    slice x1, local copies, waits for them, and re-layouts, spectrum(): weights[layer]  14.9 us
  transfers between devices with their start and end apart: 4, of which 2 were waited for; matrix products, arithmetic and copies ran while one was open for 7% of the time, Pallas kernels for 0%

profile of v1, /device:TPU:1, one launch (start us, length us, event | category | flops | bytes accessed | tf_op | source)
XLA Modules:
  0.0 339.5 jit_solution(10948864533402942763)
XLA Ops:
  0.0 0.8 multiply_bitcast_fusion
  1.1 1.1 convolution_convert_fusion
  2.2 1.2 copy.46
  3.4 11.5 %all-to-all-start = ((bf16[128,16,128]{2,1,0:T(8,128)(2,1)}), bf16[128,16,128]{2,1,0:T(8,128)(2,1)S(1)}, u32[]{:S(2)}, u32[]{:S(2)}) async-start(bf16[128,16,128]{2,1,0:T(8,128)(2,1)} %copy.46), calls=%async_computation | async-start | bytes 1048576 | tf_op jit(solution)/shard_map/all_to_all | solution.py:354
  15.5 37.4 %all-gather.1 = s32[128,2,128]{2,1,0:T(2,128)S(1)} all-gather(s32[1,2,128]{2,1,0:T(2,128)S(1)} %add_bitcast_fusion), channel_id=2, replica_groups=mesh['slab'=64,'pencil'=2] {'slab','pencil'}, dimensions={0}, use_global_device_ids=true | all-gather | bytes 132096 | tf_op jit(solution)/shard_map/all_gather | solution.py:362
  52.9 1.6 fusion.10
  54.6 0.7 reshape.120.lt_ref
  55.4 0.8 copy-done.3
  56.2 45.9 %encode.1 = (f32[64,128,128]{2,1,0:T(8,128)}, f32[128,8,128]{2,1,0:T(8,128)}) custom-call(bf16[128,16,128]{2,1,0:T(8,128)(2,1)} %copy-done.3, s32[16,16,128]{2,1,0:T(8,128)} %bitcast.58, s32[128,1,256]{2,1,0:T(1,128)} %reshape.120.lt_ref, bf16[128,256]{1,0:T(8,128)(2,1)} %constant.110.clone.yf_ref, bf16[256,256]{1,0:T(8,128)(2,1)} %constant.111.clone.zf_ref), custom_call_target="tpu_custom_call" | custom-call | tf_op jit(solution)/shard_map/encode/pallas_call | solution.py:312
  102.1 4.7 %all-to-all-start.1 = ((f32[128,8,128]{2,1,0:T(8,128)}), f32[128,8,128]{2,1,0:T(8,128)S(1)}, u32[]{:S(2)}, u32[]{:S(2)}) async-start(f32[128,8,128]{2,1,0:T(8,128)} %get-tuple-element.9), calls=%async_computation.1 | async-start | bytes 1048576 | tf_op jit(solution)/shard_map/all_to_all | solution.py:354
  106.8 14.9 %fusion.16 = (bf16[1,8,32,2,64,64]{5,4,3,2,1,0:T(8,128)(2,1)}, bf16[1,8,32,2,64,64]{5,4,3,2,1,0:T(8,128)(2,1)}) fusion(bf16[2,8,32,2,64,64]{5,4,3,2,1,0:T(8,128)(2,1)} %param.16), kind=kLoop, calls=%fused_computation.48 | loop fusion | bytes 16777216 | tf_op jit(solution)/shard_map/slice | solution.py:382
  121.7 0.8 copy-done.2
  122.5 24.7 %spectrum0.1 = f32[1024,128]{1,0:T(8,128)} custom-call(f32[1024,128]{1,0:T(8,128)} %bitcast.54, bf16[8,32,128,64]{3,2,1,0:T(8,128)(2,1)} %bitcast.50, bf16[128,256]{1,0:T(8,128)(2,1)} %constant.112.clone.xf_ref, bf16[128,192]{1,0:T(8,128)(2,1)} %constant.113.clone.xi_ref), custom_call_target="tpu_custom_call" | custom-call | tf_op jit(solution)/shard_map/spectrum0/pallas_call | solution.py:312
  147.2 9.2 %all-to-all-start.2 = ((f32[128,8,128]{2,1,0:T(8,128)}), f32[128,8,128]{2,1,0:T(8,128)S(1)}, u32[]{:S(2)}, u32[]{:S(2)}) async-start(f32[128,8,128]{2,1,0:T(8,128)} %bitcast.52), calls=%async_computation.2 | async-start | bytes 1048576 | tf_op jit(solution)/shard_map/all_to_all | solution.py:354
  156.5 0.6 pad_maximum_fusion.skip2_ref
  157.1 12.8 %all-to-all-done.2.rx_ref = f32[128,8,128]{2,1,0:T(8,128)S(1)} async-done(((f32[128,8,128]{2,1,0:T(8,128)}), f32[128,8,128]{2,1,0:T(8,128)S(1)}, u32[]{:S(2)}, u32[]{:S(2)}) %all-to-all-start.2) | async-done | bytes 524320 | tf_op jit(solution)/shard_map/all_to_all | solution.py:354
  169.9 0.8 copy-done.1
  170.7 46.2 %middle.1 = (f32[64,128,128]{2,1,0:T(8,128)}, f32[128,8,128]{2,1,0:T(8,128)}) custom-call(f32[128,8,128]{2,1,0:T(8,128)} %copy-done.1, f32[64,128,128]{2,1,0:T(8,128)} %get-tuple-element.10.field_ref, bf16[256,128]{1,0:T(8,128)(2,1)} %pad_maximum_fusion.skip2_ref, bf16[128,192]{1,0:T(8,128)(2,1)} %constant.114.clone.zi_ref, ...), custom_call_target="tpu_custom_call" | custom-call | tf_op jit(solution)/shard_map/middle/pallas_call | solution.py:312
  216.9 19.2 %all_to_all.30 = f32[128,8,128]{2,1,0:T(8,128)} all-to-all(f32[128,8,128]{2,1,0:T(8,128)} %get-tuple-element.11), channel_id=1, replica_groups=mesh['slab'=64,'pencil'=2] {'slab','pencil'}, dimensions={0} | all-to-all | bytes 1048576 | tf_op jit(solution)/shard_map/all_to_all | solution.py:354
  236.2 24.9 %spectrum1.1 = f32[1024,128]{1,0:T(8,128)} custom-call(f32[1024,128]{1,0:T(8,128)} %bitcast.55, bf16[8,32,128,64]{3,2,1,0:T(8,128)(2,1)} %bitcast.49, bf16[128,256]{1,0:T(8,128)(2,1)} %constant.112.clone.xf_ref, bf16[128,192]{1,0:T(8,128)(2,1)} %constant.113.clone.xi_ref), custom_call_target="tpu_custom_call" | custom-call | tf_op jit(solution)/shard_map/spectrum1/pallas_call | solution.py:312
  261.0 3.8 %all-to-all-start.4 = ((f32[128,8,128]{2,1,0:T(8,128)}), f32[128,8,128]{2,1,0:T(8,128)S(1)}, u32[]{:S(2)}, u32[]{:S(2)}) async-start(f32[128,8,128]{2,1,0:T(8,128)} %bitcast.53), calls=%async_computation.4 | async-start | bytes 1048576 | tf_op jit(solution)/shard_map/all_to_all | solution.py:354
  264.8 1.2 reshape_reshape.3
  266.0 2.0 copy.64
  268.3 1.1 reshape.133.iet_ref
  269.4 0.6 pad_maximum_fusion.1.skip2_ref
  270.0 8.5 %all-to-all-done.4.rx_ref = f32[128,8,128]{2,1,0:T(8,128)S(1)} async-done(((f32[128,8,128]{2,1,0:T(8,128)}), f32[128,8,128]{2,1,0:T(8,128)S(1)}, u32[]{:S(2)}, u32[]{:S(2)}) %all-to-all-start.4) | async-done | bytes 524320 | tf_op jit(solution)/shard_map/all_to_all | solution.py:354
  278.5 0.8 copy-done.4
  279.3 39.0 %final.1 = bf16[128,16,128]{2,1,0:T(8,128)(2,1)} custom-call(f32[128,8,128]{2,1,0:T(8,128)} %copy-done.4, f32[64,128,128]{2,1,0:T(8,128)} %get-tuple-element.12.field_ref, bf16[256,128]{1,0:T(8,128)(2,1)} %pad_maximum_fusion.1.skip2_ref, bf16[128,192]{1,0:T(8,128)(2,1)} %constant.114.clone.zi_ref, bf16[128,192]{1,0:T(8,128)(2,1)} %constant.115.clone.yi_ref, ...), custom_call_target="tpu_custom_call" | custom-call | tf_op jit(solution)/shard_map/final/pallas_call | solution.py:312
  318.3 18.6 %all_to_all.31 = bf16[128,16,128]{2,1,0:T(8,128)(2,1)S(1)} all-to-all(bf16[128,16,128]{2,1,0:T(8,128)(2,1)} %final.1), channel_id=1, replica_groups=mesh['slab'=64,'pencil'=2] {'slab','pencil'}, dimensions={0} | all-to-all | bytes 1048576 | tf_op jit(solution)/shard_map/all_to_all | solution.py:354
  336.9 0.5 copy.53
  337.4 1.1 fusion.3
  338.5 1.0 copy.65
  (31 shorter events, 1.4 us)
Async XLA Ops:
  0.0 1.1 copy-start
  2.2 12.8 %copy-start.7 = (s32[32,4]{0,1:T(4,128)S(1)}, s32[32,4]{0,1:T(4,128)}, u32[]{:S(2)}) copy-start(s32[32,4]{0,1:T(4,128)} %param.15) | copy-start | bytes 1540
  2.2 13.0 %copy-start.8 = (s32[32,4]{0,1:T(4,128)S(1)}, s32[32,4]{0,1:T(4,128)}, u32[]{:S(2)}) copy-start(s32[32,4]{0,1:T(4,128)} %param.14) | copy-start | bytes 1540
  3.4 52.0 %all-to-all-start = ((bf16[128,16,128]{2,1,0:T(8,128)(2,1)}), bf16[128,16,128]{2,1,0:T(8,128)(2,1)S(1)}, u32[]{:S(2)}, u32[]{:S(2)}) async-start(bf16[128,16,128]{2,1,0:T(8,128)(2,1)} %copy.46), calls=%async_computation | async-start | bytes 1048576 | tf_op jit(solution)/shard_map/all_to_all | solution.py:354
  55.4 0.8 copy-start.3
  102.1 19.6 %all-to-all-start.1 = ((f32[128,8,128]{2,1,0:T(8,128)}), f32[128,8,128]{2,1,0:T(8,128)S(1)}, u32[]{:S(2)}, u32[]{:S(2)}) async-start(f32[128,8,128]{2,1,0:T(8,128)} %get-tuple-element.9), calls=%async_computation.1 | async-start | bytes 1048576 | tf_op jit(solution)/shard_map/all_to_all | solution.py:354
  121.7 0.8 copy-start.2
  122.5 33.9 %copy-start.6 = (bf16[2,64,64]{2,1,0:T(8,128)(2,1)S(1)}, bf16[2,64,64]{2,1,0:T(8,128)(2,1)}, u32[]{:S(2)}) copy-start(bf16[2,64,64]{2,1,0:T(8,128)(2,1)} %param.17) | copy-start | bytes 49156
  147.2 22.8 %all-to-all-start.2 = ((f32[128,8,128]{2,1,0:T(8,128)}), f32[128,8,128]{2,1,0:T(8,128)S(1)}, u32[]{:S(2)}, u32[]{:S(2)}) async-start(f32[128,8,128]{2,1,0:T(8,128)} %bitcast.52), calls=%async_computation.2 | async-start | bytes 1048576 | tf_op jit(solution)/shard_map/all_to_all | solution.py:354
  169.9 0.8 copy-start.1
  261.0 17.5 %all-to-all-start.4 = ((f32[128,8,128]{2,1,0:T(8,128)}), f32[128,8,128]{2,1,0:T(8,128)S(1)}, u32[]{:S(2)}, u32[]{:S(2)}) async-start(f32[128,8,128]{2,1,0:T(8,128)} %bitcast.53), calls=%async_computation.4 | async-start | bytes 1048576 | tf_op jit(solution)/shard_map/all_to_all | solution.py:354
  266.0 2.0 copy-start.5
  278.5 0.8 copy-start.4

commit v2 on v1

--- a/solution.py
+++ b/solution.py
@@ -167,17 +167,18 @@
     rhs = jnp.concatenate([jnp.where(low, half, 0.0), jnp.where(low, 0.0, half)], 0).astype(BF)
     lanes = lax.broadcasted_iota(jnp.int32, (256, G), 1)
     hot = jnp.where(ls[:, j:j + 1] == lanes, 1.0, 0.0).astype(BF)
-    return dot(hot, rhs).astype(BF)
-
-
-def block_sums(rows2_ref, iet_ref, out_ref):
+    return dot(hot, rhs)
+
+
+def block_sums(rows2_ref, ie_ref, out_ref):
     def body(sg, _):
-        codes = iet_ref[sg]
-        rows = lax.broadcasted_iota(jnp.int32, (256, 256), 0)
+        codes = ie_ref[sg]
+        rows = lax.broadcasted_iota(jnp.int32, (256, G), 0)
         acc = jnp.zeros((256, G), F32)
         for k in range(8):
-            hot = jnp.where(codes[:, k * 256:(k + 1) * 256] == rows, 1.0, 0.0).astype(BF)
-            acc = acc + dot(hot, rows2_ref[sg, k * 16:(k + 1) * 16].reshape(256, G))
+            hot = [jnp.where(codes[i:i + 1, :] == rows, 1.0, 0.0).astype(BF) for i in (2 * k, 2 * k + 1)]
+            part = rows2_ref[pl.ds(pl.multiple_of(sg * 2048 + k * 256, 256), 256), :].astype(BF)
+            acc = acc + dot(jnp.concatenate(hot, 1), part)
         acc = acc + swap(acc)
         out = jnp.where(lane_lo((G, G)), acc[:G], acc[G:]).astype(BF)
         out_ref[pl.ds(sg * 8, 8)] = out.reshape(8, 16, G)
@@ -202,19 +203,6 @@
     return jnp.concatenate([re, im], 1)
 
 
-def encode_kernel(r_ref, ie_ref, lt_ref, yf_ref, zf_ref, field_ref, send_ref, msg_ref, rows_ref, a_ref):
-    unpack_messages(r_ref, msg_ref)
-    expand(msg_ref, ie_ref, rows_ref)
-
-    def per_slab(slab, _):
-        plane = jnp.concatenate([scatter_lines(rows_ref, lt_ref, 2 * slab), scatter_lines(rows_ref, lt_ref, 2 * slab + 1)], 0)
-        field_ref[slab] = plane
-        y_forward(yf_ref[...], plane, a_ref, slab)
-        return 0
-    lax.fori_loop(0, 64, per_slab, 0)
-    forward_modes(zf_ref, a_ref, send_ref)
-
-
 def forward_modes(zf_ref, a_ref, send_ref):
     def per_ky(ky, _):
         send_ref[pl.ds(ky * 4, 4)] = z_forward(zf_ref[...], a_ref, ky).reshape(4, 8, G)
@@ -229,95 +217,141 @@
     lax.fori_loop(0, M, per_ky, 0)
 
 
-def middle_kernel(rx_ref, field_ref, skip2_ref, zi_ref, yi_ref, yf_ref, zf_ref, out_ref, send_ref, iz_ref, a_ref):
-    inverse_modes(rx_ref, zi_ref, iz_ref)
-
-    def per_slab(slab, _):
-        plane = y_inverse_act(yi_ref[...], skip2_ref[...], iz_ref, field_ref[slab], slab)
-        out_ref[slab] = plane
-        y_forward(yf_ref[...], plane, a_ref, slab)
-        return 0
-    lax.fori_loop(0, 64, per_slab, 0)
-    forward_modes(zf_ref, a_ref, send_ref)
-
-
-def final_kernel(rx_ref, field_ref, skip2_ref, zi_ref, yi_ref, ls_ref, iet_ref, out_ref, iz_ref, rows2_ref):
-    inverse_modes(rx_ref, zi_ref, iz_ref)
-
-    def per_group(g, _):
-        ls = ls_ref[g]
-        for i in range(4):
-            slab = g * 4 + i
-            plane = y_inverse_act(yi_ref[...], skip2_ref[...], iz_ref, field_ref[slab], slab)
-            for p in range(2):
-                got = gather_lines(plane[64 * p:64 * p + 64], ls, 2 * i + p)
-                rows2_ref[:, 2 * slab + p, :, :] = got.reshape(16, 16, G)
-        return 0
-    lax.fori_loop(0, 16, per_group, 0)
-    block_sums(rows2_ref, iet_ref, out_ref)
-
-
-def spectrum_kernel(rx_ref, w_ref, xf_ref, xi_ref, out_ref, gs_ref, gr_ref, hs_ref, hr_ref, sems):
+def net_kernel(msg_in, codes_in, w_hbm, skip2_ref, yf_ref, zf_ref, xf_ref, xi_ref, zi_ref, yi_ref, out_ref,
+               recv_ref, codes_ref, send_ref, rx_ref, back_ref, sums_ref, gs_ref, gr_ref, hs_ref, hr_ref,
+               w_ref, msg_ref, ie_ref, line_ref, lt_ref, rows_ref, rows2_ref, field_ref, a_ref, iz_ref,
+               sems, group_sems, w_sems):
     slab = lax.axis_index("slab")
     pencil = lax.axis_index("pencil")
+    me = slab * 2 + pencil
     q = lax.rem(slab, 2) * 2 + pencil
     base = slab - lax.rem(slab, 2)
+
+    def partner(i):
+        d = lax.rem(me + i, NDEV)
+        return d, (lax.div(d, 2), lax.rem(d, 2))
 
     def peer(i):
         other = lax.rem(q + i, 4)
         return other, (base + lax.div(other, 2), lax.rem(other, 2))
 
     barrier = pltpu.get_barrier_semaphore()
-    for i in range(1, 4):
-        pl.semaphore_signal(barrier, inc=1, device_id=peer(i)[1], device_id_type=MESH)
-
-    rows = rx_ref.shape[0]
-
-    def fwd(kz, _):
-        plane = rx_ref[pl.ds(kz, G, stride=8), :]
-        gs_ref[:, kz] = x_forward(xf_ref[...], plane).reshape(4, 8, G)
-        return 0
-    lax.fori_loop(0, 8, fwd, 0)
+
+    def greet(i, _):
+        pl.semaphore_signal(barrier, inc=1, device_id=partner(i)[1], device_id_type=MESH)
+        return 0
+    lax.fori_loop(1, NDEV, greet, 0)
+    loads = [pltpu.make_async_copy(w_hbm.at[l], w_ref.at[l], w_sems.at[l]) for l in range(2)]
+    for load in loads:
+        load.start()
+    pl.semaphore_wait(barrier, NDEV - 1)
+
+    def local(src, dst, st):
+        return pltpu.make_async_copy(src.at[me] if src.shape[0] == NDEV else src, dst.at[me], sems.at[st, 2])
+
+    def send_all(src, dst, st):
+        local(src, dst, st).start()
+
+        def one(i, _):
+            d, did = partner(i)
+            part = src.at[d] if src.shape[0] == NDEV else src
+            pltpu.make_async_remote_copy(part, dst.at[me], sems.at[st, 0], sems.at[st, 1], device_id=did, device_id_type=MESH).start()
+            return 0
+        lax.fori_loop(1, NDEV, one, 0)
+
+    def wait_all(src, dst, st):
+        local(src, dst, st).wait()
+        rest = dst.at[pl.ds(0, NDEV - 1)]
+        pltpu.make_async_copy(rest, rest, sems.at[st, 0]).wait()
+        pltpu.make_async_copy(rest, rest, sems.at[st, 1]).wait()
 
     def exchange(src, dst, st):
-        local = pltpu.make_async_copy(src.at[q], dst.at[q], sems.at[st, 2])
-        local.start()
-        if st == 0:
-            pl.semaphore_wait(barrier, 3)
+        own = pltpu.make_async_copy(src.at[q], dst.at[q], group_sems.at[st, 2])
+        own.start()
         for i in range(1, 4):
             other, did = peer(i)
-            pltpu.make_async_remote_copy(src.at[other], dst.at[q], sems.at[st, 0], sems.at[st, 1], device_id=did, device_id_type=MESH).start()
-        local.wait()
+            pltpu.make_async_remote_copy(src.at[other], dst.at[q], group_sems.at[st, 0], group_sems.at[st, 1],
+                                         device_id=did, device_id_type=MESH).start()
+        own.wait()
         three = pl.ds(0, 3)
-        pltpu.make_async_copy(src.at[three], src.at[three], sems.at[st, 0]).wait()
-        pltpu.make_async_copy(dst.at[three], dst.at[three], sems.at[st, 1]).wait()
-
-    exchange(gs_ref, gr_ref, 0)
-
-    def modes(kz, _):
-        g, k = lax.div(kz, 8), lax.rem(kz, 8)
-        hs_ref[g, k] = mode_product(gr_ref[g, k], w_ref, kz)
-        return 0
-    lax.fori_loop(0, M, modes, 0)
-    exchange(hs_ref, hr_ref, 1)
-
-    def inv(kz, _):
-        out_ref[pl.ds(kz, G, stride=8), :] = mode_inverse(xi_ref[...], hr_ref[:, kz].reshape(M, G))
-        return 0
-    lax.fori_loop(0, 8, inv, 0)
-
-
-def call(kernel, outs, args, scratch, name, **params):
-    vm = pl.BlockSpec(memory_space=pltpu.VMEM)
-    return pl.pallas_call(
-        kernel,
-        out_shape=[jax.ShapeDtypeStruct(s, d) for s, d in outs],
-        in_specs=[vm] * len(args),
-        out_specs=[vm] * len(outs),
-        scratch_shapes=scratch,
-        compiler_params=pltpu.CompilerParams(vmem_limit_bytes=VLIM, **params),
-        name=name,
-    )(*args)
+        pltpu.make_async_copy(src.at[three], src.at[three], group_sems.at[st, 0]).wait()
+        pltpu.make_async_copy(dst.at[three], dst.at[three], group_sems.at[st, 1]).wait()
+
+    send_all(codes_in, codes_ref, 0)
+    send_all(msg_in, recv_ref, 1)
+    wait_all(codes_in, codes_ref, 0)
+    codes = codes_ref[...].reshape(256, G)
+    s8 = lax.rem(lax.div(lax.broadcasted_iota(jnp.int32, (256, G), 0), 2), 8)
+    block = lax.shift_right_arithmetic(codes, 7)
+    kpos = lax.shift_left(lax.shift_right_arithmetic(block, 4), 7) + s8 * 16 + (block & 15)
+    line = jnp.where(codes >= 0, codes & 127, -1)
+    ie_ref[...] = jnp.where(codes >= 0, kpos, -1).reshape(16, 16, G)
+    line_ref[...] = line
+    lt_ref[...] = line.T.reshape(NDEV, 1, 256)
+    wait_all(msg_in, recv_ref, 1)
+
+    unpack_messages(recv_ref, msg_ref)
+    expand(msg_ref, ie_ref, rows_ref)
+
+    def first(s, _):
+        plane = jnp.concatenate([scatter_lines(rows_ref, lt_ref, 2 * s), scatter_lines(rows_ref, lt_ref, 2 * s + 1)], 0)
+        field_ref[s] = plane
+        y_forward(yf_ref[...], plane, a_ref, s)
+        return 0
+    lax.fori_loop(0, 64, first, 0)
+
+    for layer in range(2):
+        st = 2 + 2 * layer
+        forward_modes(zf_ref, a_ref, send_ref)
+        rx = rx_ref.at[layer]
+        send_all(send_ref, rx, st)
+        wait_all(send_ref, rx, st)
+        gs, gr, hs, hr = gs_ref, gr_ref.at[layer], hs_ref, hr_ref.at[layer]
+
+        def fwd(kz, _):
+            plane = rx.reshape(NDEV * 8, G)[pl.ds(kz, G, stride=8), :]
+            gs[:, kz] = x_forward(xf_ref[...], plane).reshape(4, 8, G)
+            return 0
+        lax.fori_loop(0, 8, fwd, 0)
+        exchange(gs, gr, 2 * layer)
+        loads[layer].wait()
+
+        def modes(kz, _):
+            g, k = lax.div(kz, 8), lax.rem(kz, 8)
+            hs[g, k] = mode_product(gr[g, k], w_ref.at[layer], kz)
+            return 0
+        lax.fori_loop(0, M, modes, 0)
+        exchange(hs, hr, 2 * layer + 1)
+
+        def inv(kz, _):
+            send_ref.reshape(NDEV * 8, G)[pl.ds(kz, G, stride=8), :] = mode_inverse(xi_ref[...], hr[:, kz].reshape(M, G))
+            return 0
+        lax.fori_loop(0, 8, inv, 0)
+        back = back_ref.at[layer]
+        send_all(send_ref, back, st + 1)
+        wait_all(send_ref, back, st + 1)
+        inverse_modes(back, zi_ref, iz_ref)
+        if layer == 0:
+            def middle(s, _):
+                plane = y_inverse_act(yi_ref[...], skip2_ref[0], iz_ref, field_ref[s], s)
+                field_ref[s] = plane
+                y_forward(yf_ref[...], plane, a_ref, s)
+                return 0
+            lax.fori_loop(0, 64, middle, 0)
+        else:
+            def final(g, _):
+                ls = pltpu.roll(line_ref[...], lax.rem(NDEV - 8 * g, NDEV), 1)
+                for i in range(4):
+                    s = g * 4 + i
+                    plane = y_inverse_act(yi_ref[...], skip2_ref[1], iz_ref, field_ref[s], s)
+                    for p in range(2):
+                        rows2_ref[pl.ds(2 * s + p, 256, stride=G), :] = gather_lines(plane[64 * p:64 * p + 64], ls, 2 * i + p)
+                return 0
+            lax.fori_loop(0, 16, final, 0)
+
+    block_sums(rows2_ref, ie_ref, sums_ref)
+    send_all(sums_ref, out_ref, 6)
+    wait_all(sums_ref, out_ref, 6)
 
 
 def kernel_rows(coords):
@@ -337,65 +371,38 @@
     return jnp.stack([first, second], 0)
 
 
-def route_tables(codes):
-    s8 = (jnp.arange(NDEV, dtype=jnp.int32) % 8)[:, None, None]
-    block = codes // G
-    kpos = jnp.where(codes >= 0, (block // 16) * 128 + s8 * 16 + block % 16, -1)
-    line = jnp.where(codes >= 0, codes % G, -1)
-    ie = kpos.reshape(16, 16, NDEV)
-    iet = ie.transpose(0, 2, 1).reshape(16, 1, 2048)
-    flat = line.reshape(256, NDEV)
-    lt = flat.T.reshape(NDEV, 1, 256)
-    ls = flat.reshape(256, 16, 8).transpose(1, 0, 2)
-    return ie, iet, lt, ls
-
-
-def all_to_all(v):
-    return lax.all_to_all(v, ("slab", "pencil"), split_axis=0, concat_axis=0, tiled=True)
-
-
 def per_device(point_feats, point_x, neighbour_dev, neighbour_line, spec_weight, skip_weight):
     yf, zf, xf, xi, zi, yi = [jnp.asarray(t) for t in make_tables()]
     nb = neighbour_dev.shape[0]
     feats = point_feats.reshape(nb, -1, C)
     kernel = kernel_rows(point_x.reshape(nb, -1))
-    codes = lax.all_gather(slot_tables(neighbour_dev, neighbour_line), ("slab", "pencil"), axis=0)
+    codes = slot_tables(neighbour_dev, neighbour_line)
     message = jnp.einsum("bpx,bpc->bxc", kernel, feats, preferred_element_type=F32).astype(BF)
     outgoing = message.reshape(2, 16, G, C).transpose(2, 1, 0, 3).reshape(G, 16, 2 * C)
-    arrived = all_to_all(outgoing)
-    ie, iet, lt, ls = route_tables(codes)
     zero = jnp.zeros((C, C), BF)
-    sk = [jnp.block([[w, zero], [zero, w]]) for w in skip_weight]
-    skip2 = [jnp.concatenate([s, s], 0) for s in sk]
+    skip2 = jnp.stack([jnp.concatenate([jnp.block([[w, zero], [zero, w]])] * 2, 0) for w in skip_weight])
     weights = spec_weight.reshape(2, 8, M, 2 * C, C)
-
-    mode_shape = ((NDEV, 8, G), F32)
-    field_shape = ((64, G, G), F32)
-    field, send = call(
-        encode_kernel, [field_shape, mode_shape], [arrived, ie, lt, yf, zf],
-        [pltpu.VMEM((16, 256, G), BF), pltpu.VMEM((NDEV, 256, G), BF), pltpu.VMEM((M * G, G), F32)], "encode",
-    )
-
-    def spectrum(send, layer):
-        rx = all_to_all(send).reshape(NDEV * 8, G)
-        (back,) = call(
-            spectrum_kernel, [((NDEV * 8, G), F32)], [rx, weights[layer], xf, xi],
-            [pltpu.VMEM((4, 8, 8, G), F32)] * 4 + [pltpu.SemaphoreType.DMA((2, 3))], f"spectrum{layer}",
-            collective_id=1 + layer, has_side_effects=True,
-        )
-        return all_to_all(back.reshape(NDEV, 8, G))
-
-    back = spectrum(send, 0)
-    field, send = call(
-        middle_kernel, [field_shape, mode_shape], [back, field, skip2[0], zi, yi, yf, zf],
-        [pltpu.VMEM((64 * 64, G), F32), pltpu.VMEM((M * G, G), F32)], "middle",
-    )
-    back = spectrum(send, 1)
-    (sums,) = call(
-        final_kernel, [((NDEV, 16, G), BF)], [back, field, skip2[1], zi, yi, ls, iet],
-        [pltpu.VMEM((64 * 64, G), F32), pltpu.VMEM((16, NDEV, 16, G), BF)], "final",
-    )
-    values = all_to_all(sums)
+    vm = pl.BlockSpec(memory_space=pltpu.VMEM)
+    modes = pltpu.VMEM((NDEV, 8, G), F32)
+    pair = pltpu.VMEM((2, NDEV, 8, G), F32)
+    group = pltpu.VMEM((4, 8, 8, G), F32)
+    group2 = pltpu.VMEM((2, 4, 8, 8, G), F32)
+    values = pl.pallas_call(
+        net_kernel,
+        out_shape=jax.ShapeDtypeStruct((NDEV, 16, G), BF),
+        in_specs=[vm, vm, pl.BlockSpec(memory_space=pl.ANY)] + [vm] * 7,
+        out_specs=vm,
+        scratch_shapes=[
+            pltpu.VMEM((NDEV, 16, G), BF), pltpu.VMEM((NDEV, 2, G), jnp.int32), modes, pair, pair, pltpu.VMEM((NDEV, 16, G), BF),
+            group, group2, group, group2,
+            pltpu.VMEM((2, 8, M, 2 * C, C), BF), pltpu.VMEM((16, 256, G), BF), pltpu.VMEM((16, 16, G), jnp.int32),
+            pltpu.VMEM((256, G), jnp.int32), pltpu.VMEM((NDEV, 1, 256), jnp.int32), pltpu.VMEM((NDEV, 256, G), BF),
+            pltpu.VMEM((256 * G, G), F32), pltpu.VMEM((64, G, G), F32), pltpu.VMEM((M * G, G), F32), pltpu.VMEM((64 * 64, G), F32),
+            pltpu.SemaphoreType.DMA((7, 3)), pltpu.SemaphoreType.DMA((4, 3)), pltpu.SemaphoreType.DMA((2,)),
+        ],
+        compiler_params=pltpu.CompilerParams(vmem_limit_bytes=VLIM, collective_id=1, has_side_effects=True),
+        name="net",
+    )(outgoing, codes, weights, skip2, yf, zf, xf, xi, zi, yi)
     values = values.reshape(G, 16, 2, C).transpose(2, 1, 0, 3).reshape(nb, G, C)
     out = 0.5 * jnp.einsum("bpx,bxc->bpc", kernel, values, preferred_element_type=F32)
     return out.reshape(-1, C)

time: 340 us -> 257 us (0.76)
  blocking collectives: 75.2 us -> 0 us
  Pallas kernels: 181 us -> 245 us
  starting transfers between devices: 29.2 us -> 0 us
  waiting for transfers between devices: 21.4 us -> 0 us
  local copies, waits for them, and re-layouts: 26.9 us -> 6.32 us
    pallas_call x5 -> x1, Pallas kernels: 181 us -> 245 us  [per_device(): pl.pallas_call(net_kernel, out_shape=jax.ShapeDtypeStruct((NDEV, 16, G),...]
    all_to_all x2 -> x0, blocking collectives: 37.8 us -> none  [all_to_all(): lax.all_to_all(v, ('slab', 'pencil'), split_axis=0, concat_axis=0, tiled=...]
    all_gather x1 -> x0, blocking collectives: 37.4 us -> none  [per_device(): lax.all_gather(slot_tables(neighbour_dev, neighbour_line), ('slab', 'penc...]
    all_to_all x4 -> x0, starting transfers between devices: 29.2 us -> none  [all_to_all(): lax.all_to_all(v, ('slab', 'pencil'), split_axis=0, concat_axis=0, tiled=...]
    all_to_all x4 -> x0, waiting for transfers between devices: 21.4 us -> none  [all_to_all(): lax.all_to_all(v, ('slab', 'pencil'), split_axis=0, concat_axis=0, tiled=...]
    slice x1 -> x0, local copies, waits for them, and re-layouts: 14.9 us -> none  [spectrum(): weights[layer]]
  transfers between devices with their start and end apart: 4 -> 0, of which waited for: 2 -> 0; matrix products, arithmetic and copies ran while one was open for 7% -> 0% of each run, Pallas kernels for 0% -> 0%
where the time goes in v2:
time: 257 us; the launch traced here: 256 us
  Pallas kernels  245 us (95%)
  local copies, waits for them, and re-layouts  6.32 us (2%)
    pallas_call x1, Pallas kernels, per_device(): pl.pallas_call(net_kernel, out_shape=jax.ShapeDtypeStruct((NDEV, 16, G),...  245 us

profile of v2, /device:TPU:1, one launch (start us, length us, event | category | flops | bytes accessed | tf_op | source)
XLA Modules:
  0.0 256.2 jit_solution(5911091136086480092)
XLA Ops:
  0.0 0.0 copy-start
  0.0 0.8 multiply_bitcast_fusion
  0.8 0.8 copy.35
  1.5 0.1 eq.42
  1.6 0.8 copy.36
  2.4 0.1 reshape.80
  2.5 0.1 select_reduce_fusion.1
  2.7 0.5 pad_add_fusion.codes_in
  3.2 0.7 slice_bitcast_fusion.1
  3.9 0.1 fusion.12
  4.1 0.7 pad_maximum_fusion.skip2_ref
  4.7 0.0 copy-done
  4.7 1.1 convolution_convert_fusion
  5.9 1.2 copy.37.msg_in
  7.1 245.4 %net.1 = bf16[128,16,128]{2,1,0:T(8,128)(2,1)} custom-call(bf16[128,16,128]{2,1,0:T(8,128)(2,1)} %copy.37.msg_in, s32[2,128]{1,0:T(2,128)} %pad_add_fusion.codes_in, bf16[2,8,32,128,64]{4,3,2,1,0:T(8,128)(2,1)} %bitcast.38, bf16[2,256,128]{2,1,0:T(8,128)(2,1)} %pad_maximum_fusion.skip2_ref, bf16[128,256]{1,0:T(8,128)(2,1)} %constant.49.clone.yf_ref, ...), custom_call_target="tpu_custom_call" | custom-call | tf_op jit(solution)/shard_map/net/pallas_call | solution.py:390
  252.5 1.5 copy.38
  254.0 1.1 fusion.3
  255.1 1.0 copy.48
  (6 shorter events, 0.1 us)
Async XLA Ops:
  0.0 4.7 %copy-start = (bf16[4096,64]{0,1:T(8,128)(2,1)S(1)}, bf16[4096,64]{0,1:T(8,128)(2,1)}, u32[]{:S(2)}) copy-start(bf16[4096,64]{0,1:T(8,128)(2,1)} %param.12) | copy-start | bytes 1572868

commit v3 on v2

v3 whole, which is shorter than its diff:
```python
import jax
import jax.numpy as jnp
import numpy as np
from jax import lax
from jax.experimental import pallas as pl
from jax.experimental.pallas import tpu as pltpu
from jax.sharding import PartitionSpec as P

G = 128
C = 64
M = 32
NDEV = 128
MESH = pl.DeviceIdType.MESH
BF = jnp.bfloat16
F32 = jnp.float32
VLIM = 60 * 1024 * 1024


def trig(cells):
    waves = np.arange(M) - M // 2
    ang = ((cells[:, None] * waves[None, :]) % G) * (2.0 * np.pi / G)
    return np.cos(ang), np.sin(ang)


def split_np(t):
    hi = np.asarray(t, np.float32).astype(jnp.bfloat16)
    lo = (np.asarray(t, np.float64) - hi.astype(np.float64)).astype(np.float32).astype(jnp.bfloat16)
    return hi, lo


def tall(t):
    hi, lo = split_np(t)
    return np.concatenate([np.concatenate([hi, hi], 1), np.concatenate([lo, np.zeros_like(lo)], 1)], 0)


def wide(t):
    hi, lo = split_np(t)
    return np.concatenate([hi, hi, lo], 1)


def make_tables():
    cos, sin = trig(np.arange(G))
    yf = tall(np.concatenate([cos.T, -sin.T], 0))
    zf = []
    for z1 in range(2):
        c, s = trig(2 * np.arange(G // 2) + z1)
        zf.append(tall(np.concatenate([np.concatenate([c.T, s.T], 1), np.concatenate([-s.T, c.T], 1)], 0)))
    zf = np.concatenate(zf, 0)
    xf = tall(np.concatenate([cos.T, sin.T], 0))
    xi = wide(np.concatenate([cos, sin], 1) / float(G) ** 3)
    zi = wide(np.concatenate([np.concatenate(trig(2 * np.arange(G // 2) + z1), 1) for z1 in range(2)], 0))
    yi = wide(np.concatenate([cos, -sin], 1))
    return yf, zf, xf, xi, zi, yi


ROWS_STRIDE = 72
A_STRIDE = 136
IZ_STRIDE = 72
MSG_STRIDE = 24
cat = jnp.concatenate


def split2(v):
    hi = v.astype(BF)
    return hi, (v - hi.astype(F32)).astype(BF)


def dot(a, b):
    return jnp.dot(a, b, preferred_element_type=F32)


def tdot(a, b):
    return lax.dot_general(a, b, (((0,), (0,)), ((), ())), preferred_element_type=F32)


def lane_lo(shape):
    return lax.broadcasted_iota(jnp.int32, shape, 1) < C


def swap(v):
    return pltpu.roll(v, C, 1)


def lanes(v, n):
    return [v[:, i * G:(i + 1) * G] for i in range(n)]


def stack2(planes):
    parts = [split2(p) for p in planes]
    return cat([cat([h for h, _ in parts], 1), cat([l for _, l in parts], 1)], 0)


def stack3(planes):
    parts = [split2(p) for p in planes]
    hi = cat([h for h, _ in parts], 1)
    return cat([hi, cat([l for _, l in parts], 1), hi], 0)


def hot_rows(row, n):
    return jnp.where(row == lax.broadcasted_iota(jnp.int32, (n, row.shape[1]), 0), 1.0, 0.0).astype(BF)


def y_forward(yf, planes, a_ref, slab):
    out = dot(yf, stack2(planes))
    out = out[:2 * M] + out[2 * M:]
    for i, o in enumerate(lanes(out, len(planes))):
        a_ref[pl.ds(slab + i, M, stride=A_STRIDE), :] = o[:M]
        a_ref[pl.ds(slab + i + 64, M, stride=A_STRIDE), :] = o[M:]


def z_forward(zf, planes):
    out = dot(zf, stack2(planes))
    first = out[:64] + out[64:128]
    second = out[128:192] + out[192:]
    low = lane_lo((M, G))
    res = []
    for o0, o1 in zip(lanes(first, len(planes)), lanes(second, len(planes))):
        res.append(jnp.where(low, o0[:M], o1[M:]) + swap(jnp.where(low, o0[M:], o1[:M])))
    return res


def x_forward(xf, planes):
    out = dot(xf, stack2(planes))
    out = out[:64] + out[64:]
    low = lane_lo((M, G))
    res = []
    for o in lanes(out, len(planes)):
        rot = swap(o[M:])
        res.append(o[:M] + jnp.where(low, rot, -rot))
    return res


def rotated(modes):
    rot = swap(modes)
    return cat([modes, jnp.where(lane_lo(modes.shape), -rot, rot)], 0)


def mode_inverse(table, modes):
    return lanes(dot(table, stack3([rotated(m) for m in modes])), len(modes))


def z_inverse(zi, modes, iz_ref, ky):
    low = lane_lo((64, G))
    for i, o in enumerate(mode_inverse(zi, modes)):
        o0, o1 = o[:64], o[64:]
        iz_ref[pl.ds(ky + i, 64, stride=IZ_STRIDE), :] = jnp.where(low, o0, swap(o1))
        iz_ref[pl.ds(ky + i + M, 64, stride=IZ_STRIDE), :] = jnp.where(low, swap(o0), o1)


def gelu(v):
    k = 0.7978845608028654
    return 0.5 * v * (1.0 + jnp.tanh(k * (v + 0.044715 * (v * v * v))))


def y_inverse_act(yi, skip2, rows, planes):
    spectral = lanes(dot(yi, stack3(rows)), len(planes))
    parts = [split2(p) for p in planes]
    skipped = dot(cat([cat([h, l], 1) for h, l in parts], 0), skip2)
    return [gelu(spectral[i] + skipped[i * G:(i + 1) * G]) for i in range(len(planes))]


def message_pair(px_ref, feats_ref, b2):
    cells = lax.broadcasted_iota(jnp.int32, (G, G), 0).astype(F32)
    out = []
    for b1 in range(2):
        off = px_ref[pl.ds(b1 * 16 + b2, 1), :] * float(G) - cells
        k = jnp.exp(-off * off / (2.0 * 0.5 * 0.5)).astype(BF)
        out.append(dot(k, feats_ref[b1 * 16 + b2]))
    return cat(out, 1)


def slot_codes(dev, line):
    lane = lax.broadcasted_iota(jnp.int32, (32, G), 1)
    blocks = lax.broadcasted_iota(jnp.int32, (32, G), 0) * G
    none = 32 * G
    rows = []
    for p in range(2):
        owner = (lane & 63) * 2 + p
        first = jnp.full((32, G), none, jnp.int32)
        last = jnp.full((32, G), -1, jnp.int32)
        for t in range(4):
            hit = dev[:, t:t + 1] == owner
            code = blocks + line[:, t:t + 1]
            first = jnp.minimum(first, jnp.where(hit, code, none))
            last = jnp.maximum(last, jnp.where(hit, code, -1))
        first = jnp.min(first, axis=0, keepdims=True)
        last = jnp.max(last, axis=0, keepdims=True)
        second = jnp.where(last == first, -1, last)
        first = jnp.where(first == none, -1, first)
        rows.append(jnp.where(lane[:1] < 64, first, second))
    return cat(rows, 0)


def source_hot(codes):
    block = lax.shift_right_arithmetic(codes, 7)
    return cat([hot_rows(block[0:1], 32), hot_rows(block[1:2], 32)], 0)


def expand(msg, codes):
    low = lane_lo((16, G))
    zero = jnp.zeros((16, G), F32)
    m = msg.astype(F32)
    w = swap(m)
    both = cat([jnp.where(low, m, zero), jnp.where(low, w, zero), jnp.where(low, zero, w), jnp.where(low, zero, m)], 0)
    return tdot(source_hot(codes), both.astype(BF))


def block_sum(codes, rows):
    low = lane_lo((16, G))
    o = dot(source_hot(codes), rows.astype(BF))
    return (jnp.where(low, o[:16], o[48:]) + swap(jnp.where(low, o[16:32], o[32:48]))).astype(BF)


def slab_hot(lt_ref, slab):
    return cat([hot_rows(cat([lt_ref[p, slab], lt_ref[p, 64 + slab]], 1), G) for p in range(2)], 0)


def scatter_plane(lt_ref, rows_ref, slab):
    low = lane_lo((64, G))
    out = dot(slab_hot(lt_ref, slab), rows_ref[pl.ds(slab, 256, stride=ROWS_STRIDE), :].astype(BF))
    return cat([jnp.where(low, out[:64], swap(out[64:128])), jnp.where(low, swap(out[128:192]), out[192:])], 0)


def gather_plane(lt_ref, plane, slab):
    low = lane_lo((64, G))
    zero = jnp.zeros((64, G), F32)
    a, b = plane[:64], plane[64:]
    rhs = cat([jnp.where(low, a, zero), jnp.where(low, swap(a), zero), jnp.where(low, zero, swap(b)), jnp.where(low, zero, b)], 0)
    return tdot(slab_hot(lt_ref, slab), rhs.astype(BF))


def mode_product(f8s, w_ref, kz):
    low = lane_lo((8, G))
    row = lax.rem(lax.broadcasted_iota(jnp.int32, (32, G), 0), 8)
    res = []
    for t, f8 in enumerate(f8s):
        a = jnp.where(low, f8, -f8)
        b = swap(f8)
        ah, bh = a.astype(BF).astype(F32), b.astype(BF).astype(F32)
        lhs = cat([ah, a - ah, bh, b - bh], 0)
        acc = None
        for j in range(0, 8, 2):
            left = cat([jnp.where(row == j, lhs, 0.0).astype(BF), jnp.where(row == j + 1, lhs, 0.0).astype(BF)], 1)
            o = dot(left, cat([w_ref[j, kz + t], w_ref[j + 1, kz + t]], 0))
            acc = o if acc is None else acc + o
        res.append(cat([acc[0:8] + acc[8:16], acc[16:24] + acc[24:32]], 1))
    return res


U = 8


def net_kernel(px_ref, feats_ref, dev_ref, line_ref, w_hbm, skip_ref, yf_ref, zf_ref, xf_ref, xi_ref, zi_ref, yi_ref, out_ref,
               msg32_ref, msg_ref, recv_ref, my_codes_ref, codes_ref, send_ref, rx_ref, back_ref, sums_ref, gs_ref, gr_ref, hs_ref, hr_ref,
               w_ref, skip2_ref, lt_ref, rows_ref, field_ref, a_ref, iz_ref,
               send_sems, recv_sems, local_sems, group_send, group_recv, w_sems):
    slab = lax.axis_index("slab")
    pencil = lax.axis_index("pencil")
    me = slab * 2 + pencil
    mine = lax.div(me, 32)
    inner = lax.rem(me, 32)
    q = lax.rem(slab, 2) * 2 + pencil
    base = slab - lax.rem(slab, 2)

    def coords(d):
        return lax.div(d, 2), lax.rem(d, 2)

    barrier = pltpu.get_barrier_semaphore()

    def greet(i, _):
        pl.semaphore_signal(barrier, inc=1, device_id=coords(lax.rem(me + i, NDEV)), device_id_type=MESH)
        return 0
    lax.fori_loop(1, NDEV, greet, 0)
    loads = [pltpu.make_async_copy(w_hbm.at[l], w_ref.at[l], w_sems.at[l]) for l in range(2)]
    for load in loads:
        load.start()

    my_codes_ref[...] = slot_codes(dev_ref[...], line_ref[...])
    for l in range(2):
        w = skip_ref[l].astype(F32)
        zero = jnp.zeros((C, C), F32)
        block = cat([cat([w, zero], 1), cat([zero, w], 1)], 0).astype(BF)
        skip2_ref[l, :G, :] = block
        skip2_ref[l, G:, :] = block

    def make_messages(i, _):
        outs = [message_pair(px_ref, feats_ref, i * 4 + u) for u in range(4)]
        for u in range(4):
            msg32_ref[pl.ds(i * 4 + u, G, stride=MSG_STRIDE), :] = outs[u]
        return 0
    lax.fori_loop(0, 4, make_messages, 0)

    def pack_messages(i, _):
        for u in range(16):
            x = i * 16 + u
            msg_ref[x] = msg32_ref[pl.ds(pl.multiple_of(x * MSG_STRIDE, 8), 16), :].astype(BF)
        return 0
    lax.fori_loop(0, 8, pack_messages, 0)
    pl.semaphore_wait(barrier, NDEV - 1)

    def chunk(src, d):
        return src.at[d] if src.shape[0] == NDEV else src

    def local(src, dst, st):
        return pltpu.make_async_copy(chunk(src, me), dst.at[me], local_sems.at[st])

    def send_group(src, dst, st, t):
        group = lax.rem(mine + t, 4) * 32
        if t == 0:
            local(src, dst, st).start()

        def one(i, _):
            d = group + lax.rem(inner + i, 32)
            pltpu.make_async_remote_copy(chunk(src, d), dst.at[me], send_sems.at[st], recv_sems.at[st, t],
                                         device_id=coords(d), device_id_type=MESH).start()
            return 0
        lax.fori_loop(1 if t == 0 else 0, 32, one, 0)

    def wait_group(src, dst, st, t):
        if t == 0:
            local(src, dst, st).wait()
        part = dst.at[pl.ds(0, 31 if t == 0 else 32)]
        pltpu.make_async_copy(part, part, recv_sems.at[st, t]).wait()

    def wait_sends(dst, st):
        part = dst.at[pl.ds(0, NDEV - 1)]
        pltpu.make_async_copy(part, part, send_sems.at[st]).wait()

    def peer(i):
        other = lax.rem(q + i, 4)
        return other, (base + lax.div(other, 2), lax.rem(other, 2))

    def send_peer(src, dst, st, i):
        other, did = peer(i)
        return pltpu.make_async_remote_copy(src.at[other], dst.at[q], group_send.at[st, i], group_recv.at[st, i],
                                            device_id=did, device_id_type=MESH)

    def own_part(src, dst, st):
        return pltpu.make_async_copy(src.at[q], dst.at[q], group_recv.at[st, 0])

    for t in range(4):
        send_group(my_codes_ref, codes_ref, 0, t)
    for t in range(4):
        send_group(msg_ref, recv_ref, 1, t)
    for t in range(4):
        wait_group(my_codes_ref, codes_ref, 0, t)
    for p in range(2):
        codes = codes_ref[:, p, :]
        lt_ref[p] = jnp.where(codes >= 0, codes & 127, -1).T.reshape(G, 1, G)

    for t in range(4):
        wait_group(msg_ref, recv_ref, 1, t)
        start = lax.rem(mine + 4 - t, 4) * 32

        def expand_some(i, _):
            s0 = start + i * 16
            outs = [expand(recv_ref[s0 + u], codes_ref[s0 + u]) for u in range(16)]
            for u in range(16):
                for k in range(2):
                    rows_ref[pl.ds(pl.multiple_of((k * G + s0 + u) * ROWS_STRIDE, 8), 64), :] = outs[u][64 * k:64 * k + 64]
            return 0
        lax.fori_loop(0, 2, expand_some, 0)

    def first(g, _):
        s0 = g * U
        planes = [scatter_plane(lt_ref, rows_ref, s0 + i) for i in range(U)]
        for i in range(U):
            field_ref[s0 + i] = planes[i]
        y_forward(yf_ref[...], planes, a_ref, s0)
        return 0
    lax.fori_loop(0, 64 // U, first, 0)
    wait_sends(codes_ref, 0)
    wait_sends(recv_ref, 1)

    for layer in range(2):
        st = 2 + 2 * layer
        rx, back = rx_ref.at[layer], back_ref.at[layer]
        gs, gr, hs, hr = gs_ref, gr_ref.at[layer], hs_ref, hr_ref.at[layer]
        for t in range(4):
            ky = lax.rem(mine + t, 4) * 8
            outs = z_forward(zf_ref[...], [a_ref[pl.ds(pl.multiple_of((ky + i) * A_STRIDE, 8), G), :] for i in range(8)])
            for i in range(8):
                send_ref[pl.ds((ky + i) * 4, 4)] = outs[i].reshape(4, 8, G)
            send_group(send_ref, rx, st, t)
        for t in range(4):
            wait_group(send_ref, rx, st, t)
        rxf = rx.reshape(NDEV * 8, G)
        outs = x_forward(xf_ref[...], [rxf[pl.ds(kz, G, stride=8), :] for kz in range(8)])
        for kz in range(8):
            gs[:, kz] = outs[kz].reshape(4, 8, G)
        own_part(gs, gr, 2 * layer).start()
        for i in range(1, 4):
            send_peer(gs, gr, 2 * layer, i).start()
        loads[layer].wait()
        for i in range(4):
            g = lax.rem(q + i, 4)
            if i == 0:
                own_part(gs, gr, 2 * layer).wait()
            else:
                send_peer(gs, gr, 2 * layer, 4 - i).wait_recv()
            outs = mode_product([gr[g, k] for k in range(8)], w_ref.at[layer], g * 8)
            for k in range(8):
                hs[g, k] = outs[k]
            if i == 0:
                own_part(hs, hr, 2 * layer + 1).start()
            else:
                send_peer(hs, hr, 2 * layer + 1, i).start()
        wait_sends(rx, st)
        own_part(hs, hr, 2 * layer + 1).wait()
        for i in range(1, 4):
            send_peer(hs, hr, 2 * layer + 1, i).wait_recv()
        outs = mode_inverse(xi_ref[...], [hr[:, kz].reshape(M, G) for kz in range(8)])
        for kz in range(8):
            send_ref.reshape(NDEV * 8, G)[pl.ds(kz, G, stride=8), :] = outs[kz]
        for t in range(4):
            send_group(send_ref, back, st + 1, t)
        for i in range(1, 4):
            send_peer(gs, gr, 2 * layer, i).wait_send()
            send_peer(hs, hr, 2 * layer + 1, i).wait_send()
        for t in range(4):
            wait_group(send_ref, back, st + 1, t)
            ky = lax.rem(mine + 4 - t, 4) * 8
            z_inverse(zi_ref[...], [back[pl.ds((ky + i) * 4, 4)].reshape(M, G) for i in range(8)], iz_ref, ky)
        wait_sends(back, st + 1)

        def activate(s0):
            rows = [iz_ref[pl.ds(pl.multiple_of((s0 + i) * IZ_STRIDE, 8), 64), :] for i in range(U)]
            return y_inverse_act(yi_ref[...], skip2_ref[layer], rows, [field_ref[s0 + i] for i in range(U)])

        if layer == 0:
            def middle(g, _):
                planes = activate(g * U)
                for i in range(U):
                    field_ref[g * U + i] = planes[i]
                y_forward(yf_ref[...], planes, a_ref, g * U)
                return 0
            lax.fori_loop(0, 64 // U, middle, 0)
        else:
            def final(g, _):
                planes = activate(g * U)
                outs = [gather_plane(lt_ref, planes[i], g * U + i) for i in range(U)]
                for i in range(U):
                    rows_ref[pl.ds(g * U + i, 256, stride=ROWS_STRIDE), :] = outs[i]
                return 0
            lax.fori_loop(0, 64 // U, final, 0)

    for t in range(4):
        start = lax.rem(mine + t, 4) * 32

        def sum_some(i, _):
            s0 = start + i * 16
            outs = []
            for u in range(16):
                rows = [rows_ref[pl.ds(pl.multiple_of((k * G + s0 + u) * ROWS_STRIDE, 8), 64), :] for k in range(2)]
                outs.append(block_sum(codes_ref[s0 + u], cat(rows, 0)))
            for u in range(16):
                sums_ref[s0 + u] = outs[u]
            return 0
        lax.fori_loop(0, 2, sum_some, 0)
        send_group(sums_ref, out_ref, 6, t)
    for t in range(4):
        wait_group(sums_ref, out_ref, 6, t)
    wait_sends(out_ref, 6)


def kernel_rows(coords):
    offset_x = coords[..., None] * G - jnp.arange(G, dtype=F32)
    return jnp.exp(-offset_x * offset_x / (2.0 * 0.5 * 0.5)).astype(BF)


def per_device(point_feats, point_x, neighbour_dev, neighbour_line, spec_weight, skip_weight):
    tables = [jnp.asarray(t) for t in make_tables()]
    nb = neighbour_dev.shape[0]
    px = point_x.reshape(nb, G)
    feats = point_feats.reshape(nb, G, C)
    weights = spec_weight.reshape(2, 8, M, 2 * C, C)
    vm = pl.BlockSpec(memory_space=pltpu.VMEM)
    chunks = pltpu.VMEM((NDEV, 16, G), BF)
    modes = pltpu.VMEM((NDEV, 8, G), F32)
    pair = pltpu.VMEM((2, NDEV, 8, G), F32)
    group = pltpu.VMEM((4, 8, 8, G), F32)
    group2 = pltpu.VMEM((2, 4, 8, 8, G), F32)
    dma = pltpu.SemaphoreType.DMA
    values = pl.pallas_call(
        net_kernel,
        out_shape=jax.ShapeDtypeStruct((NDEV, 16, G), BF),
        in_specs=[vm] * 4 + [pl.BlockSpec(memory_space=pl.ANY)] + [vm] * 7,
        out_specs=vm,
        scratch_shapes=[
            pltpu.VMEM((G * MSG_STRIDE, G), F32), chunks, chunks, pltpu.VMEM((2, G), jnp.int32), pltpu.VMEM((NDEV, 2, G), jnp.int32),
            modes, pair, pair, chunks, group, group2, group, group2,
            pltpu.VMEM((2, 8, M, 2 * C, C), BF), pltpu.VMEM((2, 2 * G, G), BF), pltpu.VMEM((2, G, 1, G), jnp.int32),
            pltpu.VMEM((256 * ROWS_STRIDE, G), F32), pltpu.VMEM((64, G, G), F32),
            pltpu.VMEM((M * A_STRIDE, G), F32), pltpu.VMEM((64 * IZ_STRIDE, G), F32),
            dma((7,)), dma((7, 4)), dma((7,)), dma((4, 4)), dma((4, 4)), dma((2,)),
        ],
        compiler_params=pltpu.CompilerParams(vmem_limit_bytes=VLIM, collective_id=1, has_side_effects=True),
        name="net",
    )(px, feats, neighbour_dev, neighbour_line, weights, skip_weight, *tables)
    values = values.reshape(G, 16, 2, C).transpose(2, 1, 0, 3).reshape(nb, G, C)
    out = 0.5 * jnp.einsum("bpx,bxc->bpc", kernel_rows(px), values, preferred_element_type=F32)
    return out.reshape(-1, C)


def solution(mesh):
    both = ("slab", "pencil")
    in_specs = (P(both, None), P(both), P(both, None), P(both, None), P(None, both, None, None, None, None), P())
    return jax.shard_map(per_device, mesh=mesh, in_specs=in_specs, out_specs=P(both, None), check_vma=False)
```

time: 257 us -> 130 us (0.51)
  Pallas kernels: 245 us -> 120 us
    pallas_call x1, Pallas kernels: 245 us -> 120 us  [per_device(): pl.pallas_call(net_kernel, out_shape=jax.ShapeDtypeStruct((NDEV, 16, G),...]
    unnamed x4 -> x3, local copies, waits for them, and re-layouts: 1.53 us -> 5.07 us
where the time goes in v3:
time: 130 us; the launch traced here: 129 us
  Pallas kernels  120 us (92%)
  local copies, waits for them, and re-layouts  7.61 us (6%)
    pallas_call x1, Pallas kernels, per_device(): pl.pallas_call(net_kernel, out_shape=jax.ShapeDtypeStruct((NDEV, 16, G),...  120 us
    unnamed x3, local copies, waits for them, and re-layouts  5.07 us

profile of v3, /device:TPU:1, one launch (start us, length us, event | category | flops | bytes accessed | tf_op | source)
XLA Modules:
  0.0 129.4 jit_solution(1777899512439024960)
XLA Ops:
  0.0 1.4 %copy.23.dev_ref = s32[32,4]{1,0:T(8,128)} copy(s32[32,4]{0,1:T(4,128)} %param.14) | data formatting | bytes 1024 | tf_op args[2]
  1.4 1.4 %copy.24.line_ref = s32[32,4]{1,0:T(8,128)} copy(s32[32,4]{0,1:T(4,128)} %param.15) | data formatting | bytes 1024 | tf_op args[3]
  2.7 0.7 broadcast_multiply_fusion
  3.4 2.4 %copy.22 = bf16[4096,64]{1,0:T(8,128)(2,1)} copy(bf16[4096,64]{0,1:T(8,128)(2,1)} %param.12) | data formatting | bytes 1048576 | tf_op args[0]
  5.8 120.0 %net.1 = bf16[128,16,128]{2,1,0:T(8,128)(2,1)} custom-call(f32[32,128]{1,0:T(8,128)} %bitcast.18, bf16[32,128,64]{2,1,0:T(8,128)(2,1)} %bitcast.15, s32[32,4]{1,0:T(8,128)} %copy.23.dev_ref, s32[32,4]{1,0:T(8,128)} %copy.24.line_ref, bf16[2,8,32,128,64]{4,3,2,1,0:T(8,128)(2,1)} %bitcast.14, bf16[2,64,64]{2,1,0:T(8,128)(2,1)} %skip_ref.1, ...), custom_call_target="tpu_custom_call" | custom-call | tf_op jit(solution)/shard_map/net/pallas_call | solution.py:484
  125.8 1.5 %copy.25 = bf16[128,16,128]{0,2,1:T(8,128)(2,1)S(1)} copy(bf16[128,16,128]{2,1,0:T(8,128)(2,1)} %net.1) | data formatting | bytes 1048576 | tf_op jit(solution)/shard_map/net/pallas_call | solution.py:484
  127.3 1.1 fusion.3
  128.4 1.0 copy.30
  (1 shorter events, 0.0 us)

commit v4 on v3

--- a/solution.py
+++ b/solution.py
@@ -139,12 +139,12 @@
     return lanes(dot(table, stack3([rotated(m) for m in modes])), len(modes))
 
 
-def z_inverse(zi, modes, iz_ref, ky):
+def z_inverse(zi, modes, iz_ref, kys):
     low = lane_lo((64, G))
-    for i, o in enumerate(mode_inverse(zi, modes)):
+    for ky, o in zip(kys, mode_inverse(zi, modes)):
         o0, o1 = o[:64], o[64:]
-        iz_ref[pl.ds(ky + i, 64, stride=IZ_STRIDE), :] = jnp.where(low, o0, swap(o1))
-        iz_ref[pl.ds(ky + i + M, 64, stride=IZ_STRIDE), :] = jnp.where(low, swap(o0), o1)
+        iz_ref[pl.ds(ky, 64, stride=IZ_STRIDE), :] = jnp.where(low, o0, swap(o1))
+        iz_ref[pl.ds(ky + M, 64, stride=IZ_STRIDE), :] = jnp.where(low, swap(o0), o1)
 
 
 def gelu(v):
@@ -165,7 +165,8 @@
     for b1 in range(2):
         off = px_ref[pl.ds(b1 * 16 + b2, 1), :] * float(G) - cells
         k = jnp.exp(-off * off / (2.0 * 0.5 * 0.5)).astype(BF)
-        out.append(dot(k, feats_ref[b1 * 16 + b2]))
+        feats = feats_ref[:, pl.ds(pl.multiple_of((b1 * 16 + b2) * G, G), G)]
+        out.append(lax.dot_general(k, feats, (((1,), (1,)), ((), ())), preferred_element_type=F32))
     return cat(out, 1)
 
 
@@ -251,16 +252,25 @@
 
 
 def net_kernel(px_ref, feats_ref, dev_ref, line_ref, w_hbm, skip_ref, yf_ref, zf_ref, xf_ref, xi_ref, zi_ref, yi_ref, out_ref,
-               msg32_ref, msg_ref, recv_ref, my_codes_ref, codes_ref, send_ref, rx_ref, back_ref, sums_ref, gs_ref, gr_ref, hs_ref, hr_ref,
-               w_ref, skip2_ref, lt_ref, rows_ref, field_ref, a_ref, iz_ref,
+               msg32_ref, msg_ref, recv_ref, my_codes_ref, codes_ref, send_ref, rx_ref, back_ref, stage_ref, sums_ref, gs_ref, gr_ref, hs_ref, hr_ref,
+               turn_ref, w_ref, skip2_ref, lt_ref, rows_ref, field_ref, a_ref, iz_ref,
                send_sems, recv_sems, local_sems, group_send, group_recv, w_sems):
     slab = lax.axis_index("slab")
     pencil = lax.axis_index("pencil")
     me = slab * 2 + pencil
-    mine = lax.div(me, 32)
-    inner = lax.rem(me, 32)
+    my_y = lax.div(slab, 16)
+    mine = lax.rem(my_y + lax.rem(lax.div(slab, 4), 4), 4)
+    inner = my_y * 8 + lax.rem(me, 8)
     q = lax.rem(slab, 2) * 2 + pencil
     base = slab - lax.rem(slab, 2)
+
+    def member_ky(group, i):
+        y = lax.div(i, 2) if not isinstance(i, int) else i // 2
+        return y * 8 + lax.rem(group + 4 - y, 4) * 2 + i % 2
+
+    def member(group, i):
+        y = lax.div(i, 8)
+        return y * 32 + lax.rem(group + 4 - y, 4) * 8 + lax.rem(i, 8)
 
     def coords(d):
         return lax.div(d, 2), lax.rem(d, 2)
@@ -275,7 +285,11 @@
     for load in loads:
         load.start()
 
-    my_codes_ref[...] = slot_codes(dev_ref[...], line_ref[...])
+    turn_ref[...] = jnp.zeros((8, G), jnp.int32)
+    turn_ref[0:4, 0:32] = dev_ref[...]
+    turn_ref[4:8, 0:32] = line_ref[...]
+    named = turn_ref[...].T
+    my_codes_ref[...] = slot_codes(named[:32, 0:4], named[:32, 4:8])
     for l in range(2):
         w = skip_ref[l].astype(F32)
         zero = jnp.zeros((C, C), F32)
@@ -305,12 +319,12 @@
         return pltpu.make_async_copy(chunk(src, me), dst.at[me], local_sems.at[st])
 
     def send_group(src, dst, st, t):
-        group = lax.rem(mine + t, 4) * 32
+        group = lax.rem(mine + t, 4)
         if t == 0:
             local(src, dst, st).start()
 
         def one(i, _):
-            d = group + lax.rem(inner + i, 32)
+            d = member(group, lax.rem(inner + i, 32))
             pltpu.make_async_remote_copy(chunk(src, d), dst.at[me], send_sems.at[st], recv_sems.at[st, t],
                                          device_id=coords(d), device_id_type=MESH).start()
             return 0
@@ -350,14 +364,14 @@
 
     for t in range(4):
         wait_group(msg_ref, recv_ref, 1, t)
-        start = lax.rem(mine + 4 - t, 4) * 32
+        group = lax.rem(mine + 4 - t, 4)
 
         def expand_some(i, _):
-            s0 = start + i * 16
-            outs = [expand(recv_ref[s0 + u], codes_ref[s0 + u]) for u in range(16)]
-            for u in range(16):
+            who = [member(group, i * 16 + u) for u in range(16)]
+            outs = [expand(recv_ref[s], codes_ref[s]) for s in who]
+            for s, out in zip(who, outs):
                 for k in range(2):
-                    rows_ref[pl.ds(pl.multiple_of((k * G + s0 + u) * ROWS_STRIDE, 8), 64), :] = outs[u][64 * k:64 * k + 64]
+                    rows_ref[pl.ds(pl.multiple_of((k * G + s) * ROWS_STRIDE, 8), 64), :] = out[64 * k:64 * k + 64]
             return 0
         lax.fori_loop(0, 2, expand_some, 0)
 
@@ -377,15 +391,16 @@
         rx, back = rx_ref.at[layer], back_ref.at[layer]
         gs, gr, hs, hr = gs_ref, gr_ref.at[layer], hs_ref, hr_ref.at[layer]
         for t in range(4):
-            ky = lax.rem(mine + t, 4) * 8
-            outs = z_forward(zf_ref[...], [a_ref[pl.ds(pl.multiple_of((ky + i) * A_STRIDE, 8), G), :] for i in range(8)])
-            for i in range(8):
-                send_ref[pl.ds((ky + i) * 4, 4)] = outs[i].reshape(4, 8, G)
+            group = lax.rem(mine + t, 4)
+            kys = [member_ky(group, i) for i in range(8)]
+            outs = z_forward(zf_ref[...], [a_ref[pl.ds(pl.multiple_of(ky * A_STRIDE, 8), G), :] for ky in kys])
+            for ky, out in zip(kys, outs):
+                send_ref[pl.ds(ky * 4, 4)] = out.astype(BF).reshape(4, 8, G)
             send_group(send_ref, rx, st, t)
         for t in range(4):
             wait_group(send_ref, rx, st, t)
-        rxf = rx.reshape(NDEV * 8, G)
-        outs = x_forward(xf_ref[...], [rxf[pl.ds(kz, G, stride=8), :] for kz in range(8)])
+        stage_ref[...] = rx[...].reshape(NDEV * 8, G).astype(F32)
+        outs = x_forward(xf_ref[...], [stage_ref[pl.ds(kz, G, stride=8), :] for kz in range(8)])
         for kz in range(8):
             gs[:, kz] = outs[kz].reshape(4, 8, G)
         own_part(gs, gr, 2 * layer).start()
@@ -411,7 +426,8 @@
             send_peer(hs, hr, 2 * layer + 1, i).wait_recv()
         outs = mode_inverse(xi_ref[...], [hr[:, kz].reshape(M, G) for kz in range(8)])
         for kz in range(8):
-            send_ref.reshape(NDEV * 8, G)[pl.ds(kz, G, stride=8), :] = outs[kz]
+            stage_ref[pl.ds(kz, G, stride=8), :] = outs[kz]
+        send_ref[...] = stage_ref[...].astype(BF).reshape(NDEV, 8, G)
         for t in range(4):
             send_group(send_ref, back, st + 1, t)
         for i in range(1, 4):
@@ -419,8 +435,9 @@
             send_peer(hs, hr, 2 * layer + 1, i).wait_send()
         for t in range(4):
             wait_group(send_ref, back, st + 1, t)
-            ky = lax.rem(mine + 4 - t, 4) * 8
-            z_inverse(zi_ref[...], [back[pl.ds((ky + i) * 4, 4)].reshape(M, G) for i in range(8)], iz_ref, ky)
+            group = lax.rem(mine + 4 - t, 4)
+            kys = [member_ky(group, i) for i in range(8)]
+            z_inverse(zi_ref[...], [back[pl.ds(ky * 4, 4)].reshape(M, G).astype(F32) for ky in kys], iz_ref, kys)
         wait_sends(back, st + 1)
 
         def activate(s0):
@@ -445,16 +462,16 @@
             lax.fori_loop(0, 64 // U, final, 0)
 
     for t in range(4):
-        start = lax.rem(mine + t, 4) * 32
+        group = lax.rem(mine + t, 4)
 
         def sum_some(i, _):
-            s0 = start + i * 16
+            who = [member(group, i * 16 + u) for u in range(16)]
             outs = []
-            for u in range(16):
-                rows = [rows_ref[pl.ds(pl.multiple_of((k * G + s0 + u) * ROWS_STRIDE, 8), 64), :] for k in range(2)]
-                outs.append(block_sum(codes_ref[s0 + u], cat(rows, 0)))
-            for u in range(16):
-                sums_ref[s0 + u] = outs[u]
+            for s in who:
+                rows = [rows_ref[pl.ds(pl.multiple_of((k * G + s) * ROWS_STRIDE, 8), 64), :] for k in range(2)]
+                outs.append(block_sum(codes_ref[s], cat(rows, 0)))
+            for s, out in zip(who, outs):
+                sums_ref[s] = out
             return 0
         lax.fori_loop(0, 2, sum_some, 0)
         send_group(sums_ref, out_ref, 6, t)
@@ -472,12 +489,11 @@
     tables = [jnp.asarray(t) for t in make_tables()]
     nb = neighbour_dev.shape[0]
     px = point_x.reshape(nb, G)
-    feats = point_feats.reshape(nb, G, C)
     weights = spec_weight.reshape(2, 8, M, 2 * C, C)
     vm = pl.BlockSpec(memory_space=pltpu.VMEM)
     chunks = pltpu.VMEM((NDEV, 16, G), BF)
-    modes = pltpu.VMEM((NDEV, 8, G), F32)
-    pair = pltpu.VMEM((2, NDEV, 8, G), F32)
+    modes = pltpu.VMEM((NDEV, 8, G), BF)
+    pair = pltpu.VMEM((2, NDEV, 8, G), BF)
     group = pltpu.VMEM((4, 8, 8, G), F32)
     group2 = pltpu.VMEM((2, 4, 8, 8, G), F32)
     dma = pltpu.SemaphoreType.DMA
@@ -488,15 +504,15 @@
         out_specs=vm,
         scratch_shapes=[
             pltpu.VMEM((G * MSG_STRIDE, G), F32), chunks, chunks, pltpu.VMEM((2, G), jnp.int32), pltpu.VMEM((NDEV, 2, G), jnp.int32),
-            modes, pair, pair, chunks, group, group2, group, group2,
-            pltpu.VMEM((2, 8, M, 2 * C, C), BF), pltpu.VMEM((2, 2 * G, G), BF), pltpu.VMEM((2, G, 1, G), jnp.int32),
+            modes, pair, pair, pltpu.VMEM((NDEV * 8, G), F32), chunks, group, group2, group, group2,
+            pltpu.VMEM((8, G), jnp.int32), pltpu.VMEM((2, 8, M, 2 * C, C), BF), pltpu.VMEM((2, 2 * G, G), BF), pltpu.VMEM((2, G, 1, G), jnp.int32),
             pltpu.VMEM((256 * ROWS_STRIDE, G), F32), pltpu.VMEM((64, G, G), F32),
             pltpu.VMEM((M * A_STRIDE, G), F32), pltpu.VMEM((64 * IZ_STRIDE, G), F32),
             dma((7,)), dma((7, 4)), dma((7,)), dma((4, 4)), dma((4, 4)), dma((2,)),
         ],
         compiler_params=pltpu.CompilerParams(vmem_limit_bytes=VLIM, collective_id=1, has_side_effects=True),
         name="net",
-    )(px, feats, neighbour_dev, neighbour_line, weights, skip_weight, *tables)
+    )(px, point_feats.T, neighbour_dev.T, neighbour_line.T, weights, skip_weight, *tables)
     values = values.reshape(G, 16, 2, C).transpose(2, 1, 0, 3).reshape(nb, G, C)
     out = 0.5 * jnp.einsum("bpx,bxc->bpc", kernel_rows(px), values, preferred_element_type=F32)
     return out.reshape(-1, C)

time: 130 us -> 113 us (0.87)
  Pallas kernels: 120 us -> 109 us
  local copies, waits for them, and re-layouts: 7.61 us -> 2.54 us
    pallas_call x1, Pallas kernels: 120 us -> 109 us  [per_device(): pl.pallas_call(net_kernel, out_shape=jax.ShapeDtypeStruct((NDEV, 16, G),...]
    unnamed x3 -> x0, local copies, waits for them, and re-layouts: 5.07 us -> none
where the time goes in v4:
time: 113 us
  Pallas kernels  109 us (96%)
  local copies, waits for them, and re-layouts  2.54 us (2%)
    pallas_call x1, Pallas kernels, per_device(): pl.pallas_call(net_kernel, out_shape=jax.ShapeDtypeStruct((NDEV, 16, G),...  109 us

profile of v4, /device:TPU:1, one launch (start us, length us, event | category | flops | bytes accessed | tf_op | source)
XLA Modules:
  0.0 113.2 jit_solution(1855835665316251889)
XLA Ops:
  0.0 0.7 broadcast_multiply_fusion
  0.7 108.8 %net.1 = bf16[128,16,128]{2,1,0:T(8,128)(2,1)} custom-call(f32[32,128]{1,0:T(8,128)} %bitcast.20, bf16[64,4096]{1,0:T(8,128)(2,1)} %bitcast.18, s32[4,32]{1,0:T(4,128)} %bitcast.21, s32[4,32]{1,0:T(4,128)} %bitcast.22, bf16[2,8,32,128,64]{4,3,2,1,0:T(8,128)(2,1)} %bitcast.16, bf16[2,64,64]{2,1,0:T(8,128)(2,1)} %skip_ref.1, ...), custom_call_target="tpu_custom_call" | custom-call | tf_op jit(solution)/shard_map/net/pallas_call | solution.py:500
  109.5 1.5 %copy.16 = bf16[128,16,128]{0,2,1:T(8,128)(2,1)S(1)} copy(bf16[128,16,128]{2,1,0:T(8,128)(2,1)} %net.1) | data formatting | bytes 1048576 | tf_op jit(solution)/shard_map/net/pallas_call | solution.py:500
  111.0 1.1 fusion.3
  112.2 1.0 copy.21
  (1 shorter events, 0.0 us)

commit v5 on v4

--- a/solution.py
+++ b/solution.py
@@ -152,11 +152,15 @@
     return 0.5 * v * (1.0 + jnp.tanh(k * (v + 0.044715 * (v * v * v))))
 
 
-def y_inverse_act(yi, skip2, rows, planes):
-    spectral = lanes(dot(yi, stack3(rows)), len(planes))
+def skip_map(skip2, planes):
     parts = [split2(p) for p in planes]
-    skipped = dot(cat([cat([h, l], 1) for h, l in parts], 0), skip2)
-    return [gelu(spectral[i] + skipped[i * G:(i + 1) * G]) for i in range(len(planes))]
+    out = dot(cat([cat([h, l], 1) for h, l in parts], 0), skip2)
+    return [out[i * G:(i + 1) * G] for i in range(len(planes))]
+
+
+def y_inverse_act(yi, rows, skipped):
+    spectral = lanes(dot(yi, stack3(rows)), len(rows))
+    return [gelu(a + b) for a, b in zip(spectral, skipped)]
 
 
 def message_pair(px_ref, feats_ref, b2):
@@ -192,23 +196,22 @@
     return cat(rows, 0)
 
 
-def source_hot(codes):
-    block = lax.shift_right_arithmetic(codes, 7)
-    return cat([hot_rows(block[0:1], 32), hot_rows(block[1:2], 32)], 0)
-
-
-def expand(msg, codes):
+def source_hot(blk_ref, s):
+    return cat([hot_rows(blk_ref[p, pl.ds(s, 1), :], 32) for p in range(2)], 0)
+
+
+def expand(msg, blk_ref, s):
     low = lane_lo((16, G))
     zero = jnp.zeros((16, G), F32)
     m = msg.astype(F32)
     w = swap(m)
     both = cat([jnp.where(low, m, zero), jnp.where(low, w, zero), jnp.where(low, zero, w), jnp.where(low, zero, m)], 0)
-    return tdot(source_hot(codes), both.astype(BF))
-
-
-def block_sum(codes, rows):
+    return tdot(source_hot(blk_ref, s), both.astype(BF))
+
+
+def block_sum(rows, blk_ref, s):
     low = lane_lo((16, G))
-    o = dot(source_hot(codes), rows.astype(BF))
+    o = dot(source_hot(blk_ref, s), rows.astype(BF))
     return (jnp.where(low, o[:16], o[48:]) + swap(jnp.where(low, o[16:32], o[32:48]))).astype(BF)
 
 
@@ -230,150 +233,167 @@
     return tdot(slab_hot(lt_ref, slab), rhs.astype(BF))
 
 
-def mode_product(f8s, w_ref, kz):
+def pack_weights(w_ref, pack_ref):
+    def body(kz4, _):
+        for j in range(4):
+            cols = [cat([w_ref[2 * j, kz4 * 4 + e], w_ref[2 * j + 1, kz4 * 4 + e]], 0) for e in range(4)]
+            pack_ref[kz4, j] = cat(cols, 1)
+        return 0
+    lax.fori_loop(0, 8, body, 0)
+
+
+def mode_product(f8s, pack_ref, kz4):
     low = lane_lo((8, G))
     row = lax.rem(lax.broadcasted_iota(jnp.int32, (32, G), 0), 8)
-    res = []
-    for t, f8 in enumerate(f8s):
+    lhs = []
+    for f8 in f8s:
         a = jnp.where(low, f8, -f8)
         b = swap(f8)
         ah, bh = a.astype(BF).astype(F32), b.astype(BF).astype(F32)
-        lhs = cat([ah, a - ah, bh, b - bh], 0)
+        lhs.append(cat([ah, a - ah, bh, b - bh], 0))
+    res = []
+    for n in range(len(f8s) // 4):
         acc = None
-        for j in range(0, 8, 2):
-            left = cat([jnp.where(row == j, lhs, 0.0).astype(BF), jnp.where(row == j + 1, lhs, 0.0).astype(BF)], 1)
-            o = dot(left, cat([w_ref[j, kz + t], w_ref[j + 1, kz + t]], 0))
+        for j in range(4):
+            left = [cat([jnp.where(row == 2 * j + e, l, 0.0).astype(BF) for e in range(2)], 1) for l in lhs[4 * n:4 * n + 4]]
+            o = dot(cat(left, 0), pack_ref[kz4 + n, j])
             acc = o if acc is None else acc + o
-        res.append(cat([acc[0:8] + acc[8:16], acc[16:24] + acc[24:32]], 1))
+        for e in range(4):
+            o = acc[32 * e:32 * e + 32, G * (e // 2):G * (e // 2) + G]
+            re, im = o[0:8] + o[8:16], o[16:24] + o[24:32]
+            res.append(jnp.where(low, re, swap(im)) if e % 2 == 0 else jnp.where(low, swap(re), im))
     return res
 
 
 U = 8
+OFFSETS = (((2, 2), (1, 2), (2, 1), (3, 2)), ((2, 3), (0, 2), (2, 0), (1, 1)), ((1, 3), (3, 1), (3, 3), (0, 1)), ((0, 3), (1, 0), (3, 0), (0, 0)))
+FWD = F32
+INV = BF
 
 
 def net_kernel(px_ref, feats_ref, dev_ref, line_ref, w_hbm, skip_ref, yf_ref, zf_ref, xf_ref, xi_ref, zi_ref, yi_ref, out_ref,
-               msg32_ref, msg_ref, recv_ref, my_codes_ref, codes_ref, send_ref, rx_ref, back_ref, stage_ref, sums_ref, gs_ref, gr_ref, hs_ref, hr_ref,
-               turn_ref, w_ref, skip2_ref, lt_ref, rows_ref, field_ref, a_ref, iz_ref,
+               msg32_ref, msg_ref, recv_ref, my_codes_ref, codes_ref, fsend_ref, isend_ref, rx_ref, back_ref, stage_ref, sums_ref, gs_ref, gr_ref, hs_ref, hr_ref,
+               turn_ref, w_ref, pack_ref, skip2_ref, lt_ref, blk_ref, rows_ref, field_ref, a_ref, iz_ref,
                send_sems, recv_sems, local_sems, group_send, group_recv, w_sems):
     slab = lax.axis_index("slab")
     pencil = lax.axis_index("pencil")
     me = slab * 2 + pencil
-    my_y = lax.div(slab, 16)
-    mine = lax.rem(my_y + lax.rem(lax.div(slab, 4), 4), 4)
-    inner = my_y * 8 + lax.rem(me, 8)
+    my_y, my_x, my_z = lax.div(slab, 16), lax.rem(lax.div(slab, 4), 4), lax.rem(slab, 4)
     q = lax.rem(slab, 2) * 2 + pencil
     base = slab - lax.rem(slab, 2)
 
-    def member_ky(group, i):
-        y = lax.div(i, 2) if not isinstance(i, int) else i // 2
-        return y * 8 + lax.rem(group + 4 - y, 4) * 2 + i % 2
-
-    def member(group, i):
-        y = lax.div(i, 8)
-        return y * 32 + lax.rem(group + 4 - y, 4) * 8 + lax.rem(i, 8)
+    def column(t, i, sign):
+        dy, dx = OFFSETS[t][i]
+        return (lax.rem(my_y + 4 + sign * dy, 4) * 4 + lax.rem(my_x + 4 + sign * dx, 4)) * 4
+
+    def group_kys(t, sign):
+        return [lax.div(column(t, i, sign), 2) + h for i in range(4) for h in range(2)]
+
+    def group_devices(t, sign):
+        out = []
+        for i in range(4):
+            first = column(t, i, sign)
+            for dz in (2, 1, 3, 0):
+                chip = first + lax.rem(my_z + dz, 4)
+                out += [(chip, 1 - pencil), (chip, pencil)]
+        return out
 
     def coords(d):
         return lax.div(d, 2), lax.rem(d, 2)
 
     barrier = pltpu.get_barrier_semaphore()
 
-    def greet(i, _):
+    def greet(i):
         pl.semaphore_signal(barrier, inc=1, device_id=coords(lax.rem(me + i, NDEV)), device_id_type=MESH)
+
+    for i in range(1, 4):
+        greet(i)
+    loads = [pltpu.make_async_copy(w_hbm.at[l], w_ref.at[l], w_sems.at[l]) for l in range(2)]
+
+    def make_messages(i, _):
+        for u in range(31):
+            greet(4 + i * 31 + u)
+        outs = [message_pair(px_ref, feats_ref, i * 4 + u) for u in range(4)]
+        for u in range(4):
+            msg32_ref[pl.ds(i * 4 + u, G, stride=MSG_STRIDE), :] = outs[u]
         return 0
-    lax.fori_loop(1, NDEV, greet, 0)
-    loads = [pltpu.make_async_copy(w_hbm.at[l], w_ref.at[l], w_sems.at[l]) for l in range(2)]
-    for load in loads:
-        load.start()
-
+    lax.fori_loop(0, 4, make_messages, 0)
+
+    def pack_messages(i, _):
+        for u in range(16):
+            x = i * 16 + u
+            msg_ref[x] = msg32_ref[pl.ds(pl.multiple_of(x * MSG_STRIDE, 8), 16), :].astype(BF)
+        return 0
+    lax.fori_loop(0, 8, pack_messages, 0)
     turn_ref[...] = jnp.zeros((8, G), jnp.int32)
     turn_ref[0:4, 0:32] = dev_ref[...]
     turn_ref[4:8, 0:32] = line_ref[...]
     named = turn_ref[...].T
     my_codes_ref[...] = slot_codes(named[:32, 0:4], named[:32, 4:8])
+    pl.semaphore_wait(barrier, NDEV - 1)
+
+    def chunk(src, d):
+        return src.at[d] if src.shape[0] == NDEV else src
+
+    def local(src, dst, st):
+        return pltpu.make_async_copy(chunk(src, me), dst.at[me], local_sems.at[st])
+
+    def send_group(src, dst, st, t):
+        if t == 3:
+            local(src, dst, st).start()
+        for chip, core in group_devices(t, 1)[:31 if t == 3 else 32]:
+            pltpu.make_async_remote_copy(chunk(src, chip * 2 + core), dst.at[me], send_sems.at[st], recv_sems.at[st, t],
+                                         device_id=(chip, core), device_id_type=MESH).start()
+
+    def wait_group(src, dst, st, t):
+        if t == 3:
+            local(src, dst, st).wait()
+        part = dst.at[pl.ds(0, 31 if t == 3 else 32)]
+        pltpu.make_async_copy(part, part, recv_sems.at[st, t]).wait()
+
+    def wait_sends(dst, st):
+        part = dst.at[pl.ds(0, NDEV - 1)]
+        pltpu.make_async_copy(part, part, send_sems.at[st]).wait()
+
+    def peer(i):
+        other = lax.rem(q + i, 4)
+        return other, (base + lax.div(other, 2), lax.rem(other, 2))
+
+    def send_peer(src, dst, st, i):
+        other, did = peer(i)
+        return pltpu.make_async_remote_copy(src.at[other], dst.at[q], group_send.at[st, i], group_recv.at[st, i],
+                                            device_id=did, device_id_type=MESH)
+
+    def own_part(src, dst, st):
+        return pltpu.make_async_copy(src.at[q], dst.at[q], group_recv.at[st, 0])
+
+    for t in range(4):
+        send_group(my_codes_ref, codes_ref, 0, t)
+    for t in range(4):
+        send_group(msg_ref, recv_ref, 1, t)
     for l in range(2):
         w = skip_ref[l].astype(F32)
         zero = jnp.zeros((C, C), F32)
         block = cat([cat([w, zero], 1), cat([zero, w], 1)], 0).astype(BF)
         skip2_ref[l, :G, :] = block
         skip2_ref[l, G:, :] = block
-
-    def make_messages(i, _):
-        outs = [message_pair(px_ref, feats_ref, i * 4 + u) for u in range(4)]
-        for u in range(4):
-            msg32_ref[pl.ds(i * 4 + u, G, stride=MSG_STRIDE), :] = outs[u]
-        return 0
-    lax.fori_loop(0, 4, make_messages, 0)
-
-    def pack_messages(i, _):
-        for u in range(16):
-            x = i * 16 + u
-            msg_ref[x] = msg32_ref[pl.ds(pl.multiple_of(x * MSG_STRIDE, 8), 16), :].astype(BF)
-        return 0
-    lax.fori_loop(0, 8, pack_messages, 0)
-    pl.semaphore_wait(barrier, NDEV - 1)
-
-    def chunk(src, d):
-        return src.at[d] if src.shape[0] == NDEV else src
-
-    def local(src, dst, st):
-        return pltpu.make_async_copy(chunk(src, me), dst.at[me], local_sems.at[st])
-
-    def send_group(src, dst, st, t):
-        group = lax.rem(mine + t, 4)
-        if t == 0:
-            local(src, dst, st).start()
-
-        def one(i, _):
-            d = member(group, lax.rem(inner + i, 32))
-            pltpu.make_async_remote_copy(chunk(src, d), dst.at[me], send_sems.at[st], recv_sems.at[st, t],
-                                         device_id=coords(d), device_id_type=MESH).start()
-            return 0
-        lax.fori_loop(1 if t == 0 else 0, 32, one, 0)
-
-    def wait_group(src, dst, st, t):
-        if t == 0:
-            local(src, dst, st).wait()
-        part = dst.at[pl.ds(0, 31 if t == 0 else 32)]
-        pltpu.make_async_copy(part, part, recv_sems.at[st, t]).wait()
-
-    def wait_sends(dst, st):
-        part = dst.at[pl.ds(0, NDEV - 1)]
-        pltpu.make_async_copy(part, part, send_sems.at[st]).wait()
-
-    def peer(i):
-        other = lax.rem(q + i, 4)
-        return other, (base + lax.div(other, 2), lax.rem(other, 2))
-
-    def send_peer(src, dst, st, i):
-        other, did = peer(i)
-        return pltpu.make_async_remote_copy(src.at[other], dst.at[q], group_send.at[st, i], group_recv.at[st, i],
-                                            device_id=did, device_id_type=MESH)
-
-    def own_part(src, dst, st):
-        return pltpu.make_async_copy(src.at[q], dst.at[q], group_recv.at[st, 0])
-
-    for t in range(4):
-        send_group(my_codes_ref, codes_ref, 0, t)
-    for t in range(4):
-        send_group(msg_ref, recv_ref, 1, t)
     for t in range(4):
         wait_group(my_codes_ref, codes_ref, 0, t)
     for p in range(2):
         codes = codes_ref[:, p, :]
         lt_ref[p] = jnp.where(codes >= 0, codes & 127, -1).T.reshape(G, 1, G)
+        blk_ref[p] = lax.shift_right_arithmetic(codes, 7)
 
     for t in range(4):
         wait_group(msg_ref, recv_ref, 1, t)
-        group = lax.rem(mine + 4 - t, 4)
-
-        def expand_some(i, _):
-            who = [member(group, i * 16 + u) for u in range(16)]
-            outs = [expand(recv_ref[s], codes_ref[s]) for s in who]
+        for half in range(2):
+            who = [column(t, half * 2 + u // 8, -1) * 2 + u % 8 for u in range(16)]
+            outs = [expand(recv_ref[s], blk_ref, s) for s in who]
             for s, out in zip(who, outs):
                 for k in range(2):
                     rows_ref[pl.ds(pl.multiple_of((k * G + s) * ROWS_STRIDE, 8), 64), :] = out[64 * k:64 * k + 64]
-            return 0
-        lax.fori_loop(0, 2, expand_some, 0)
+
+    loads[0].start()
 
     def first(g, _):
         s0 = g * U
@@ -391,29 +411,33 @@
         rx, back = rx_ref.at[layer], back_ref.at[layer]
         gs, gr, hs, hr = gs_ref, gr_ref.at[layer], hs_ref, hr_ref.at[layer]
         for t in range(4):
-            group = lax.rem(mine + t, 4)
-            kys = [member_ky(group, i) for i in range(8)]
+            kys = group_kys(t, 1)
             outs = z_forward(zf_ref[...], [a_ref[pl.ds(pl.multiple_of(ky * A_STRIDE, 8), G), :] for ky in kys])
             for ky, out in zip(kys, outs):
-                send_ref[pl.ds(ky * 4, 4)] = out.astype(BF).reshape(4, 8, G)
-            send_group(send_ref, rx, st, t)
+                fsend_ref[pl.ds(ky * 4, 4)] = out.astype(FWD).reshape(4, 8, G)
+            send_group(fsend_ref, rx, st, t)
+        loads[layer].wait()
+        pack_weights(w_ref.at[layer], pack_ref)
         for t in range(4):
-            wait_group(send_ref, rx, st, t)
-        stage_ref[...] = rx[...].reshape(NDEV * 8, G).astype(F32)
-        outs = x_forward(xf_ref[...], [stage_ref[pl.ds(kz, G, stride=8), :] for kz in range(8)])
+            wait_group(fsend_ref, rx, st, t)
+        if FWD == F32:
+            by_x = rx.reshape(NDEV * 8, G)
+        else:
+            by_x = stage_ref
+            by_x[...] = rx[...].reshape(NDEV * 8, G).astype(F32)
+        outs = x_forward(xf_ref[...], [by_x[pl.ds(kz, G, stride=8), :] for kz in range(8)])
         for kz in range(8):
             gs[:, kz] = outs[kz].reshape(4, 8, G)
         own_part(gs, gr, 2 * layer).start()
         for i in range(1, 4):
             send_peer(gs, gr, 2 * layer, i).start()
-        loads[layer].wait()
         for i in range(4):
             g = lax.rem(q + i, 4)
             if i == 0:
                 own_part(gs, gr, 2 * layer).wait()
             else:
                 send_peer(gs, gr, 2 * layer, 4 - i).wait_recv()
-            outs = mode_product([gr[g, k] for k in range(8)], w_ref.at[layer], g * 8)
+            outs = mode_product([gr[g, k] for k in range(8)], pack_ref, g * 2)
             for k in range(8):
                 hs[g, k] = outs[k]
             if i == 0:
@@ -425,26 +449,36 @@
         for i in range(1, 4):
             send_peer(hs, hr, 2 * layer + 1, i).wait_recv()
         outs = mode_inverse(xi_ref[...], [hr[:, kz].reshape(M, G) for kz in range(8)])
+        by_x = isend_ref.reshape(NDEV * 8, G) if INV == F32 else stage_ref
         for kz in range(8):
-            stage_ref[pl.ds(kz, G, stride=8), :] = outs[kz]
-        send_ref[...] = stage_ref[...].astype(BF).reshape(NDEV, 8, G)
+            by_x[pl.ds(kz, G, stride=8), :] = outs[kz]
+        if INV != F32:
+            isend_ref[...] = stage_ref[...].astype(INV).reshape(NDEV, 8, G)
         for t in range(4):
-            send_group(send_ref, back, st + 1, t)
+            send_group(isend_ref, back, st + 1, t)
         for i in range(1, 4):
             send_peer(gs, gr, 2 * layer, i).wait_send()
             send_peer(hs, hr, 2 * layer + 1, i).wait_send()
+
+        def skip_some(g, _):
+            outs = skip_map(skip2_ref[layer], [field_ref[g * U + i] for i in range(U)])
+            for i in range(U):
+                field_ref[g * U + i] = outs[i]
+            return 0
+        lax.fori_loop(0, 64 // U, skip_some, 0)
         for t in range(4):
-            wait_group(send_ref, back, st + 1, t)
-            group = lax.rem(mine + 4 - t, 4)
-            kys = [member_ky(group, i) for i in range(8)]
+            wait_group(isend_ref, back, st + 1, t)
+            kys = group_kys(t, -1)
             z_inverse(zi_ref[...], [back[pl.ds(ky * 4, 4)].reshape(M, G).astype(F32) for ky in kys], iz_ref, kys)
         wait_sends(back, st + 1)
 
         def activate(s0):
             rows = [iz_ref[pl.ds(pl.multiple_of((s0 + i) * IZ_STRIDE, 8), 64), :] for i in range(U)]
-            return y_inverse_act(yi_ref[...], skip2_ref[layer], rows, [field_ref[s0 + i] for i in range(U)])
+            return y_inverse_act(yi_ref[...], rows, [field_ref[s0 + i] for i in range(U)])
 
         if layer == 0:
+            loads[1].start()
+
             def middle(g, _):
                 planes = activate(g * U)
                 for i in range(U):
@@ -462,18 +496,14 @@
             lax.fori_loop(0, 64 // U, final, 0)
 
     for t in range(4):
-        group = lax.rem(mine + t, 4)
-
-        def sum_some(i, _):
-            who = [member(group, i * 16 + u) for u in range(16)]
+        for half in range(2):
+            who = [column(t, half * 2 + u // 8, 1) * 2 + u % 8 for u in range(16)]
             outs = []
             for s in who:
                 rows = [rows_ref[pl.ds(pl.multiple_of((k * G + s) * ROWS_STRIDE, 8), 64), :] for k in range(2)]
-                outs.append(block_sum(codes_ref[s], cat(rows, 0)))
+                outs.append(block_sum(cat(rows, 0), blk_ref, s))
             for s, out in zip(who, outs):
                 sums_ref[s] = out
-            return 0
-        lax.fori_loop(0, 2, sum_some, 0)
         send_group(sums_ref, out_ref, 6, t)
     for t in range(4):
         wait_group(sums_ref, out_ref, 6, t)
@@ -492,8 +522,7 @@
     weights = spec_weight.reshape(2, 8, M, 2 * C, C)
     vm = pl.BlockSpec(memory_space=pltpu.VMEM)
     chunks = pltpu.VMEM((NDEV, 16, G), BF)
-    modes = pltpu.VMEM((NDEV, 8, G), BF)
-    pair = pltpu.VMEM((2, NDEV, 8, G), BF)
+    modes = [pltpu.VMEM((NDEV, 8, G), t) for t in (FWD, INV)] + [pltpu.VMEM((2, NDEV, 8, G), t) for t in (FWD, INV)]
     group = pltpu.VMEM((4, 8, 8, G), F32)
     group2 = pltpu.VMEM((2, 4, 8, 8, G), F32)
     dma = pltpu.SemaphoreType.DMA
@@ -504,8 +533,8 @@
         out_specs=vm,
         scratch_shapes=[
             pltpu.VMEM((G * MSG_STRIDE, G), F32), chunks, chunks, pltpu.VMEM((2, G), jnp.int32), pltpu.VMEM((NDEV, 2, G), jnp.int32),
-            modes, pair, pair, pltpu.VMEM((NDEV * 8, G), F32), chunks, group, group2, group, group2,
-            pltpu.VMEM((8, G), jnp.int32), pltpu.VMEM((2, 8, M, 2 * C, C), BF), pltpu.VMEM((2, 2 * G, G), BF), pltpu.VMEM((2, G, 1, G), jnp.int32),
+            *modes, pltpu.VMEM((NDEV * 8, G), F32), chunks, group, group2, group, group2,
+            pltpu.VMEM((8, G), jnp.int32), pltpu.VMEM((2, 8, M, 2 * C, C), BF), pltpu.VMEM((8, 4, 256, 256), BF), pltpu.VMEM((2, 2 * G, G), BF), pltpu.VMEM((2, G, 1, G), jnp.int32), pltpu.VMEM((2, G, G), jnp.int32),
             pltpu.VMEM((256 * ROWS_STRIDE, G), F32), pltpu.VMEM((64, G, G), F32),
             pltpu.VMEM((M * A_STRIDE, G), F32), pltpu.VMEM((64 * IZ_STRIDE, G), F32),
             dma((7,)), dma((7, 4)), dma((7,)), dma((4, 4)), dma((4, 4)), dma((2,)),

time: 113 us -> 110 us (0.973)
  Pallas kernels: 109 us -> 105 us
    pallas_call x1, Pallas kernels: 109 us -> 105 us  [per_device(): pl.pallas_call(net_kernel, out_shape=jax.ShapeDtypeStruct((NDEV, 16, G),...]
where the time goes in v5:
time: 110 us; the launch traced here: 109 us
  Pallas kernels  105 us (95%)
  local copies, waits for them, and re-layouts  2.54 us (2%)
  matrix products  1.13 us (1%)
    pallas_call x1, Pallas kernels, per_device(): pl.pallas_call(net_kernel, out_shape=jax.ShapeDtypeStruct((NDEV, 16, G),...  105 us

profile of v5, /device:TPU:1, one launch (start us, length us, event | category | flops | bytes accessed | tf_op | source)
XLA Modules:
  0.0 109.3 jit_solution(15710657541171264749)
XLA Ops:
  0.0 0.7 broadcast_multiply_fusion
  0.7 104.9 %net.1 = bf16[128,16,128]{2,1,0:T(8,128)(2,1)} custom-call(f32[32,128]{1,0:T(8,128)} %bitcast.20, bf16[64,4096]{1,0:T(8,128)(2,1)} %bitcast.18, s32[4,32]{1,0:T(4,128)} %bitcast.21, s32[4,32]{1,0:T(4,128)} %bitcast.22, bf16[2,8,32,128,64]{4,3,2,1,0:T(8,128)(2,1)} %bitcast.16, bf16[2,64,64]{2,1,0:T(8,128)(2,1)} %skip_ref.1, ...), custom_call_target="tpu_custom_call" | custom-call | tf_op jit(solution)/shard_map/net/pallas_call | solution.py:529
  105.6 1.5 %copy.16 = bf16[128,16,128]{0,2,1:T(8,128)(2,1)S(1)} copy(bf16[128,16,128]{2,1,0:T(8,128)(2,1)} %net.1) | data formatting | bytes 1048576 | tf_op jit(solution)/shard_map/net/pallas_call | solution.py:529
  107.1 1.1 %fusion.3 = f32[32,8,8,128]{3,2,1,0:T(8,128)S(1)} fusion(bf16[32,128,64]{1,2,0:T(8,128)(2,1)S(1)} %bitcast.19, f32[32,128]{1,0:T(8,128)S(1)} %broadcast_multiply_fusion), kind=kOutput, calls=%fused_computation.5 | convolution fusion | flops 69992448 | bytes 1589248 | tf_op jit(solution)/shard_map/bpx,bxc->bpc/dot_general | solution.py:546
  108.3 1.0 copy.21
  (1 shorter events, 0.0 us)

commit v6 on v5

--- a/solution.py
+++ b/solution.py
@@ -265,7 +265,7 @@
     return res
 
 
-U = 8
+U = 16
 OFFSETS = (((2, 2), (1, 2), (2, 1), (3, 2)), ((2, 3), (0, 2), (2, 0), (1, 1)), ((1, 3), (3, 1), (3, 3), (0, 1)), ((0, 3), (1, 0), (3, 0), (0, 0)))
 FWD = F32
 INV = BF

time: 110 us -> 107 us (0.973)
  Pallas kernels: 105 us -> 102 us
    pallas_call x1, Pallas kernels: 105 us -> 102 us  [per_device(): pl.pallas_call(net_kernel, out_shape=jax.ShapeDtypeStruct((NDEV, 16, G),...]
where the time goes in v6:
time: 107 us
  Pallas kernels  102 us (95%)
  local copies, waits for them, and re-layouts  2.54 us (2%)
  matrix products  1.13 us (1%)
    pallas_call x1, Pallas kernels, per_device(): pl.pallas_call(net_kernel, out_shape=jax.ShapeDtypeStruct((NDEV, 16, G),...  102 us

profile of v6, /device:TPU:1, one launch (start us, length us, event | category | flops | bytes accessed | tf_op | source)
XLA Modules:
  0.0 106.6 jit_solution(16386045315186919836)
XLA Ops:
  0.0 0.7 broadcast_multiply_fusion
  0.7 102.2 %net.1 = bf16[128,16,128]{2,1,0:T(8,128)(2,1)} custom-call(f32[32,128]{1,0:T(8,128)} %bitcast.20, bf16[64,4096]{1,0:T(8,128)(2,1)} %bitcast.18, s32[4,32]{1,0:T(4,128)} %bitcast.21, s32[4,32]{1,0:T(4,128)} %bitcast.22, bf16[2,8,32,128,64]{4,3,2,1,0:T(8,128)(2,1)} %bitcast.16, bf16[2,64,64]{2,1,0:T(8,128)(2,1)} %skip_ref.1, ...), custom_call_target="tpu_custom_call" | custom-call | tf_op jit(solution)/shard_map/net/pallas_call | solution.py:529
  102.9 1.5 %copy.16 = bf16[128,16,128]{0,2,1:T(8,128)(2,1)S(1)} copy(bf16[128,16,128]{2,1,0:T(8,128)(2,1)} %net.1) | data formatting | bytes 1048576 | tf_op jit(solution)/shard_map/net/pallas_call | solution.py:529
  104.4 1.1 %fusion.3 = f32[32,8,8,128]{3,2,1,0:T(8,128)S(1)} fusion(bf16[32,128,64]{1,2,0:T(8,128)(2,1)S(1)} %bitcast.19, f32[32,128]{1,0:T(8,128)S(1)} %broadcast_multiply_fusion), kind=kOutput, calls=%fused_computation.5 | convolution fusion | flops 69992448 | bytes 1589248 | tf_op jit(solution)/shard_map/bpx,bxc->bpc/dot_general | solution.py:546
  105.5 1.0 copy.21
  (1 shorter events, 0.0 us)
